TPU v7x, 512 devices: a whole 4x4x16 slice. The times are simulated.
512 devices in a mesh: dp: 64 (over z, x_lo, core), mp: 8 (over y, x_hi).
Axes of the slice: x: 4 (x_hi: 2, x_lo: 2; x = x_hi * 2 + x_lo), y: 4, z: 16, core: 2. Of those that a mesh axis runs over, the one named last changes fastest.
Arguments:
- latents: bfloat16 [512, 512, 1024], P('dp', None, 'mp'), may hold values from -16 to 16
- labels: bfloat16 [512, 512, 128], P('dp'), may hold values from -6 to 6
- slot_source: int32 [128], replicated, may hold values from 0 to 127, each once
- episode_pick: int32 [128], replicated, may hold values from 0 to 7
- window_start: int32 [128], replicated, may hold values from 0 to 256
- proj_weight: bfloat16 [1024, 6144], P('dp', 'mp')
- norm_gain: float32 [6144], P('mp'), may hold values from 0.25 to 1.75
- head_weight: bfloat16 [6144, 128], P('mp'), may hold values from -0.078125 to 0.078125
Outputs:
- grad_proj: float32 [1024, 6144], P('dp', 'mp')
- grad_head: float32 [6144, 128], P('mp')
- grad_gain: float32 [6144], P('mp')
- features: bfloat16 [32768, 6144], P('dp', 'mp')
Inputs may be any that keep to these rules, and one draw needn't show every extreme that they name: slot_source is a permutation of 0 to 127, so each shard of 8 episodes fills exactly 2 batch windows.
All inputs are finite; a program needn't handle non-finite values.
Results may differ from a plain program's by a relative error of at most 0.0065.
Values may be sent and summed in bfloat16 or wider, within the bound.
No kernel may reach another device: no remote copies, remote signals or barrier semaphores. Data moves between devices by JAX's collectives and lax.ppermute only.
A program may use at most 64 MiB of HBM per device.

v0:
```python
import math

import jax
import jax.numpy as jnp
from jax import lax
from jax.sharding import PartitionSpec as P

D = 6144
WIN = 256


EPSILON = 1e-05


def on_device(
    latents, labels, slot_source, episode_pick, window_start, proj_weight, norm_gain, head_weight
):
    groups = lax.axis_size("dp")
    position = lax.axis_index("dp")
    total_slots = slot_source.shape[0]
    slots_here = total_slots // groups
    outgoing = position * slots_here + jnp.arange(slots_here, dtype=jnp.int32)
    numbers = jnp.arange(total_slots, dtype=jnp.int32)
    matches = slot_source[None, :] == outgoing[:, None]
    chosen = jnp.sum(jnp.where(matches, numbers[None, :], 0), axis=1)
    episodes = episode_pick[chosen]
    offsets = window_start[chosen]
    zero_index = jnp.zeros((), jnp.int32)

    def cut_window(episode, offset):
        window_lat = lax.dynamic_slice(
            latents, (episode, offset, zero_index), (1, WIN, latents.shape[2])
        )[0]
        window_lab = lax.dynamic_slice(
            labels, (episode, offset, zero_index), (1, WIN, labels.shape[2])
        )[0]
        return (window_lat, window_lab)

    sent_lat, sent_lab = jax.vmap(cut_window)(episodes, offsets)
    sent_lat = lax.all_gather(sent_lat, "mp", axis=2, tiled=True)
    pieces_lat, pieces_lab = (
        lax.all_to_all(sent_lat, "dp", split_axis=1, concat_axis=0, tiled=True),
        lax.all_to_all(sent_lab, "dp", split_axis=1, concat_axis=0, tiled=True),
    )
    ordered_lat = pieces_lat[slot_source]
    ordered_lab = pieces_lab[slot_source]
    owned_lat, owned_lab = (
        lax.all_to_all(ordered_lat, "dp", split_axis=0, concat_axis=1, tiled=True),
        lax.all_to_all(ordered_lab, "dp", split_axis=0, concat_axis=1, tiled=True),
    )
    tokens_here = slots_here * WIN
    inputs = owned_lat.reshape(tokens_here, owned_lat.shape[2])
    targets = owned_lab.reshape(tokens_here, owned_lab.shape[2])
    full_proj = lax.all_gather(proj_weight, "dp", axis=0, tiled=True)
    hidden = jnp.dot(inputs, full_proj, preferred_element_type=jnp.float32)
    row_sum, row_square = lax.psum(
        (jnp.sum(hidden, axis=1), jnp.sum(hidden * hidden, axis=1)), "mp"
    )
    row_mean = row_sum / D
    variance = row_square / D - row_mean * row_mean
    row_scale = lax.rsqrt(variance + EPSILON)
    normed = (hidden - row_mean[:, None]) * row_scale[:, None]
    features = (normed * norm_gain).astype(jnp.bfloat16)
    predicted = lax.psum(
        jnp.dot(features, head_weight, preferred_element_type=jnp.float32).astype(jnp.bfloat16),
        "mp",
    ).astype(jnp.float32)
    tokens_all = tokens_here * groups
    error_grad = ((predicted - targets.astype(jnp.float32)) / math.sqrt(tokens_all)).astype(
        jnp.bfloat16
    )
    head_term = lax.dot_general(
        features, error_grad, (((0,), (0,)), ((), ())), preferred_element_type=jnp.float32
    )
    back_feat = lax.dot_general(
        error_grad, head_weight, (((1,), (1,)), ((), ())), preferred_element_type=jnp.float32
    )
    gain_term = jnp.sum(back_feat * normed, axis=0)
    grad_head, grad_gain = lax.psum((head_term, gain_term), "dp")
    back_norm = back_feat * norm_gain
    first_sum, second_sum = lax.psum(
        (jnp.sum(back_norm, axis=1), jnp.sum(back_norm * normed, axis=1)), "mp"
    )
    back_hidden = (
        row_scale[:, None]
        * (back_norm - first_sum[:, None] / D - normed * (second_sum[:, None] / D))
    ).astype(jnp.bfloat16)
    full_term = lax.dot_general(
        inputs, back_hidden, (((0,), (0,)), ((), ())), preferred_element_type=jnp.float32
    )
    grad_proj = lax.psum_scatter(full_term, "dp", scatter_dimension=0, tiled=True)
    return (grad_proj, grad_head, grad_gain, features)


def solution(mesh):
    in_specs = (
        P("dp", None, "mp"),
        P("dp", None, None),
        P(),
        P(),
        P(),
        P("dp", "mp"),
        P("mp"),
        P("mp", None),
    )
    out_specs = (P("dp", "mp"), P("mp", None), P("mp"), P("dp", "mp"))
    return jax.shard_map(
        on_device, mesh=mesh, in_specs=in_specs, out_specs=out_specs, check_vma=False
    )
```

profile of v0, /device:TPU:8, one launch (start us, length us, event | category | flops | bytes accessed | tf_op | source)
XLA Modules:
  0.0 1092.5 jit_solution(18425350361892461258)
XLA Ops:
  8.0 0.0 all-gather.6.cloned.1.call-start
  8.1 0.9 fusion.6
  9.0 1.3 gather_fusion.1
  10.3 1.3 gather_fusion
  11.6 0.7 copy.44
  12.3 2.2 gather_fusion.2
  14.6 0.0 all-gather.6.cloned.1.call-update
  14.6 71.0 %all-gather.6.cloned.1.call-done = bf16[2,256,1024]{2,0,1:T(2,128)(2,1)} async-done(((bf16[2,256,128]{2,0,1:T(2,128)(2,1)}), bf16[2,256,1024]{2,0,1:T(2,128)(2,1)}) %all-gather.6.cloned.1.call-update) | async-done | bytes 1048592 | tf_op jit(solution)/shard_map/all_gather | solution.py:40
  85.6 14.1 %all-to-all-start = ((bf16[2,256,1024]{2,0,1:T(2,128)(2,1)}), bf16[2,256,1024]{2,0,1:T(2,128)(2,1)S(1)}, u32[]{:S(2)}, u32[]{:S(2)}) async-start(bf16[2,256,1024]{2,0,1:T(2,128)(2,1)} %all-gather.6.cloned.1.call-done), calls=%async_computation | async-start | bytes 2097152 | tf_op jit(solution)/shard_map/all_to_all | solution.py:42
  99.8 0.7 copy.47
  100.5 2.2 gather_fusion.4
  102.7 53.2 %all-to-all-done = bf16[2,256,1024]{2,0,1:T(2,128)(2,1)S(1)} async-done(((bf16[2,256,1024]{2,0,1:T(2,128)(2,1)}), bf16[2,256,1024]{2,0,1:T(2,128)(2,1)S(1)}, u32[]{:S(2)}, u32[]{:S(2)}) %all-to-all-start) | async-done | bytes 1048608 | tf_op jit(solution)/shard_map/all_to_all | solution.py:42
  155.9 4.6 all-to-all-start.2
  160.5 0.5 copy.45
  161.1 2.4 gather_fusion.3
  163.4 14.1 %all-to-all-done.2 = bf16[2,256,128]{2,0,1:T(2,128)(2,1)S(1)} async-done(((bf16[2,256,128]{2,0,1:T(2,128)(2,1)}), bf16[2,256,128]{2,0,1:T(2,128)(2,1)S(1)}, u32[]{:S(2)}, u32[]{:S(2)}) %all-to-all-start.2) | async-done | bytes 131104 | tf_op jit(solution)/shard_map/all_to_all | solution.py:43
  177.5 4.7 all-to-all-start.1
  182.2 0.0 all-gather.4.cloned.1.call-start
  182.2 0.5 all-gather.4.cloned.1.call-update
  182.8 0.1 copy.48
  182.9 0.1 copy.49
  183.0 1.4 gather_fusion.5
  184.4 55.7 %all-to-all-done.1 = bf16[128,4,1024]{2,1,0:T(4,128)(2,1)S(1)} async-done(((bf16[128,4,1024]{2,1,0:T(4,128)(2,1)}), bf16[128,4,1024]{2,1,0:T(4,128)(2,1)S(1)}, u32[]{:S(2)}, u32[]{:S(2)}) %all-to-all-start.1) | async-done | bytes 1048608 | tf_op jit(solution)/shard_map/all_to_all | solution.py:48
  240.1 4.6 all-to-all-start.3
  244.7 0.0 all-reduce.5.cloned.1.call-start
  244.8 0.4 copy.54
  245.1 0.3 reshape.69
  245.4 69.4 %all-gather.4.cloned.1.call-done = bf16[1024,768]{1,0:T(8,128)(2,1)} async-done(((bf16[16,768]{1,0:T(8,128)(2,1)}), bf16[1024,768]{1,0:T(8,128)(2,1)}) %all-gather.4.cloned.1.call-update) | async-done | bytes 1572880 | tf_op jit(solution)/shard_map/all_gather | solution.py:54
  314.9 2.5 multiply_reduce_fusion.2
  317.4 21.3 %all-reduce.1 = (f32[512]{0:T(512)S(1)}, f32[512]{0:T(512)S(1)}) all-reduce(f32[512]{0:T(512)S(1)} %get-tuple-element.8, f32[512]{0:T(512)S(1)} %get-tuple-element.7), channel_id=1, replica_groups=mesh['dp'=64,'mp'=8] {'mp'}, use_global_device_ids=true, to_apply=%region_4.5 | all-reduce | flops 1024 | bytes 8192 | tf_op jit(solution)/shard_map/psum | solution.py:56
  338.7 0.3 multiply_convert_fusion.1
  339.0 0.9 copy-done.1
  339.9 1.0 convolution_convert_fusion
  340.9 0.0 all-reduce.5.cloned.1.call-update
  341.0 0.0 all-reduce.7.cloned.1.call-start
  341.1 0.2 copy.51
  341.2 91.7 %all-reduce.5.cloned.1.call-done = bf16[512,128]{1,0:T(8,128)(2,1)} async-done(((bf16[512,128]{1,0:T(8,128)(2,1)}), bf16[512,128]{1,0:T(8,128)(2,1)}) %all-reduce.5.cloned.1.call-update) | async-done | bytes 131088 | tf_op jit(solution)/shard_map/psum | solution.py:64
  432.9 2.3 fusion.14
  435.2 0.0 all-reduce.7.cloned.1.call-update
  435.2 0.0 reduce-scatter.2.cloned.1.call-start
  435.3 1.8 multiply_reduce_fusion
  437.1 19.8 %all-reduce = (f32[512]{0:T(512)S(1)}, f32[512]{0:T(512)S(1)}) all-reduce(f32[512]{0:T(512)S(1)} %get-tuple-element.5, f32[512]{0:T(512)S(1)} %get-tuple-element.6), channel_id=1, replica_groups=mesh['dp'=64,'mp'=8] {'mp'}, use_global_device_ids=true, to_apply=%region_9.10 | all-reduce | flops 1024 | bytes 8192 | tf_op jit(solution)/shard_map/psum | solution.py:81
  456.9 4.5 fusion
  461.4 0.0 reduce-scatter.2.cloned.1.call-update
  461.4 105.8 %psum.55 = f32[768]{0:T(1024)} all-reduce(f32[768]{0:T(1024)S(1)} %get-tuple-element.4), channel_id=1, replica_groups=mesh['dp'=64,'mp'=8] {'dp'}, use_global_device_ids=true, to_apply=%region_13.14 | all-reduce | flops 768 | bytes 6144 | tf_op jit(solution)/shard_map/psum | solution.py:79
  567.2 281.9 %all-reduce.7.cloned.1.call-done = f32[768,128]{1,0:T(8,128)} async-done(((f32[768,128]{1,0:T(8,128)}), f32[768,128]{1,0:T(8,128)}) %all-reduce.7.cloned.1.call-update) | async-done | bytes 393232 | tf_op jit(solution)/shard_map/psum | solution.py:79
  849.1 234.1 %reduce-scatter.2.cloned.1.call-done = f32[16,768]{1,0:T(8,128)} async-done(((f32[1024,768]{1,0:T(8,128)}), f32[16,768]{1,0:T(8,128)}) %reduce-scatter.2.cloned.1.call-update) | async-done | bytes 49168 | tf_op jit(solution)/shard_map/reduce_scatter | solution.py:91
  1083.2 1.8 copy.57
  (23 shorter events, 0.1 us)
Async XLA Ops:
  8.0 331.9 %copy-start = (bf16[768,128]{1,0:T(8,128)(2,1)S(1)}, bf16[768,128]{1,0:T(8,128)(2,1)}, u32[]{:S(2)}) copy-start(bf16[768,128]{1,0:T(8,128)(2,1)} %param.15) | copy-start | bytes 589828
  8.0 3.6 copy-start.2
  8.0 77.6 %all-gather.6.cloned.1.call-start = ((), (), s32[]{:S(2)}) async-start(), calls=%async_computation.9 | async-start | bytes 1179648 | tf_op jit(solution)/shard_map/all_gather | solution.py:40
  12.3 87.4 %copy-start.3 = (bf16[8,512,128]{2,1,0:T(8,128)(2,1)S(1)}, bf16[8,512,128]{2,1,0:T(8,128)(2,1)}, u32[]{:S(2)}) copy-start(bf16[8,512,128]{2,1,0:T(8,128)(2,1)} %param.9) | copy-start | bytes 3145732
  85.6 70.2 %all-to-all-start = ((bf16[2,256,1024]{2,0,1:T(2,128)(2,1)}), bf16[2,256,1024]{2,0,1:T(2,128)(2,1)S(1)}, u32[]{:S(2)}, u32[]{:S(2)}) async-start(bf16[2,256,1024]{2,0,1:T(2,128)(2,1)} %all-gather.6.cloned.1.call-done), calls=%async_computation | async-start | bytes 2097152 | tf_op jit(solution)/shard_map/all_to_all | solution.py:42
  99.8 60.8 %copy-start.6 = (s32[128]{0:T(128)S(1)}, s32[128]{0:T(128)}, u32[]{:S(2)}) copy-start(s32[128]{0:T(128)} %param.10) | copy-start | bytes 1540
  155.9 21.6 %all-to-all-start.2 = ((bf16[2,256,128]{2,0,1:T(2,128)(2,1)}), bf16[2,256,128]{2,0,1:T(2,128)(2,1)S(1)}, u32[]{:S(2)}, u32[]{:S(2)}) async-start(bf16[2,256,128]{2,0,1:T(2,128)(2,1)} %gather_fusion.4), calls=%async_computation.2 | async-start | bytes 262144 | tf_op jit(solution)/shard_map/all_to_all | solution.py:43
  177.5 62.6 %all-to-all-start.1 = ((bf16[128,4,1024]{2,1,0:T(4,128)(2,1)}), bf16[128,4,1024]{2,1,0:T(4,128)(2,1)S(1)}, u32[]{:S(2)}, u32[]{:S(2)}) async-start(bf16[128,4,1024]{2,1,0:T(4,128)(2,1)} %gather_fusion.3), calls=%async_computation.1 | async-start | bytes 2097152 | tf_op jit(solution)/shard_map/all_to_all | solution.py:48
  182.2 132.7 %all-gather.4.cloned.1.call-start = ((), (), s32[]{:S(2)}) async-start(), calls=%async_computation.5 | async-start | bytes 1597440 | tf_op jit(solution)/shard_map/all_gather | solution.py:54
  240.1 100.9 %all-to-all-start.3 = ((bf16[128,4,128]{2,1,0:T(4,128)(2,1)}), bf16[128,4,128]{2,1,0:T(4,128)(2,1)S(1)}, u32[]{:S(2)}, u32[]{:S(2)}) async-start(bf16[128,4,128]{2,1,0:T(4,128)(2,1)} %gather_fusion.5), calls=%async_computation.3 | async-start | bytes 262144 | tf_op jit(solution)/shard_map/all_to_all | solution.py:49
  244.7 188.2 %all-reduce.5.cloned.1.call-start = ((), (), s32[]{:S(2)}) async-start(), calls=%async_computation.6 | async-start | bytes 262144 | tf_op jit(solution)/shard_map/psum | solution.py:64
  245.4 93.3 %copy-start.5 = (f32[768]{0:T(1024)S(1)}, f32[768]{0:T(1024)}, u32[]{:S(2)}) copy-start(f32[768]{0:T(1024)} %param.14) | copy-start | bytes 9220
  339.0 0.9 copy-start.1
  341.0 508.1 %all-reduce.7.cloned.1.call-start = ((), (), s32[]{:S(2)}) async-start(), calls=%async_computation.8 | async-start | bytes 786432 | tf_op jit(solution)/shard_map/psum | solution.py:79
  432.9 2.4 copy-start.4
  435.2 647.9 %reduce-scatter.2.cloned.1.call-start = ((), (), s32[]{:S(2)}) async-start(), calls=%async_computation.7 | async-start | bytes 3194880 | tf_op jit(solution)/shard_map/reduce_scatter | solution.py:91
Sparse Core Ops, SparseCore 0:
  14.7 70.8 all-gather.5
  341.1 91.7 all-reduce.4
Sparse Core Ops, SparseCore 1:
  184.8 130.0 all-gather.3
  435.3 413.7 all-reduce.6
  852.3 230.8 reduce-scatter.1
where the time goes:
time: 1090 us
  waiting for transfers between devices  872 us (80%)
  blocking collectives  147 us (13%)
  starting transfers between devices  28.2 us (3%)
  local copies, waits for them, and re-layouts  16.4 us (2%)
  between operations  15.9 us (1%)
  matrix products  12.1 us (1%)
    psum x1, waiting for transfers between devices, on_device(): grad_head, grad_gain = lax.psum((head_term, gain_term), 'dp')  282 us
    reduce_scatter x1, waiting for transfers between devices, on_device(): lax.psum_scatter(full_term, 'dp', scatter_dimension=0, tiled=True)  234 us
    psum x1, blocking collectives, on_device(): grad_head, grad_gain = lax.psum((head_term, gain_term), 'dp')  106 us
    psum x1, waiting for transfers between devices, on_device(): lax.psum(jnp.dot(features, head_weight, preferred_element_type=jnp.float3...  91.7 us
    all_gather x1, waiting for transfers between devices, on_device(): sent_lat = lax.all_gather(sent_lat, 'mp', axis=2, tiled=True)  71 us
    all_gather x1, waiting for transfers between devices, on_device(): full_proj = lax.all_gather(proj_weight, 'dp', axis=0, tiled=True)  69.4 us
    all_to_all x1, waiting for transfers between devices, on_device(): lax.all_to_all(ordered_lat, 'dp', split_axis=0, concat_axis=1, tiled=True)  55.7 us
    all_to_all x1, waiting for transfers between devices, on_device(): lax.all_to_all(sent_lat, 'dp', split_axis=1, concat_axis=0, tiled=True)  53.2 us
  transfers between devices with their start and end apart: 9, of which 8 were waited for; matrix products, arithmetic and copies ran while one was open for 2% of the time, Pallas kernels for 0%

commit v1 on v0

v1 whole, which is shorter than its diff:
```python
import math

import jax
import jax.numpy as jnp
from jax import lax
from jax.experimental import pallas as pl
from jax.experimental.pallas import tpu as pltpu
from jax.sharding import PartitionSpec as P

D = 6144
WIN = 256
EPSILON = 1e-05
BF = jnp.bfloat16
F32 = jnp.float32

N_DP = 64
Z_GROUPS = [[z * 4 + q for z in range(16)] for q in range(4)]


def to_core(i):
    return i ^ 1


def to_xlo(i):
    return i ^ 2


def to_zl(k):
    return lambda i: (i & ~12) | ((i + 4 * k) & 12)


def to_zh(k):
    return lambda i: (i + 16 * k) % N_DP


def permute(x, target):
    return lax.ppermute(x, "dp", [(i, target(i)) for i in range(N_DP)])


def exchange(x, axis, groups=None):
    return lax.all_to_all(
        x, axis, split_axis=0, concat_axis=0, tiled=True, axis_index_groups=groups
    )


def gather(x, axis, groups=None):
    return lax.all_gather(x, axis, axis=0, tiled=True, axis_index_groups=groups)


def copies(x, n):
    return jnp.broadcast_to(x[None], (n,) + x.shape)


def take(x, index, axis):
    return lax.dynamic_index_in_dim(x, index, axis, keepdims=False)


def pair(mine, other, index):
    return jnp.where(index == 0, jnp.stack([mine, other]), jnp.stack([other, mine]))


def scatter4(blocks, index, to):
    total = take(blocks, index, 0)
    for k in (1, 2, 3):
        sent = take(blocks, (index + k) % 4, 0).astype(BF)
        total = total + permute(sent, to(k)).astype(F32)
    return total


def tie(x, y):
    return lax.optimization_barrier((x, y))


def cut_kernel(
    position_ref, slot_ref, pick_ref, start_ref, latents_ref, labels_ref,
    copies_ref, own_ref, targets_ref, lat_held, lab_held, wide, sems,
):
    shifts, moves = [], []
    for k in range(2):
        here = slot_ref[...] == position_ref[0] * 2 + k
        episode = jnp.sum(jnp.where(here, pick_ref[...], 0).astype(F32)).astype(jnp.int32)
        start = jnp.sum(jnp.where(here, start_ref[...], 0).astype(F32)).astype(jnp.int32)
        first = pl.multiple_of(jnp.minimum(start // 16, 15) * 16, 16)
        shifts.append(start - first)
        for n, (store, held) in enumerate(((latents_ref, lat_held), (labels_ref, lab_held))):
            move = pltpu.make_async_copy(
                store.at[episode, pl.ds(first, WIN + 16), :], held.at[k], sems.at[n, k]
            )
            move.start()
            moves.append(move)
    for k in range(2):
        rows = slice(k * WIN, (k + 1) * WIN)
        moves[2 * k].wait()
        wide[k] = lat_held[k].astype(F32)
        window = wide[k, pl.ds(shifts[k], WIN), :].astype(BF)
        own_ref[rows, :] = window
        for m in range(8):
            copies_ref[m, rows, :] = window
    for k in range(2):
        moves[2 * k + 1].wait()
        wide[k] = lab_held[k].astype(F32)
        targets_ref[k * WIN : (k + 1) * WIN, :] = wide[k, pl.ds(shifts[k], WIN), :]


def cut_windows(latents, labels, slot_source, episode_pick, window_start, position):
    smem = pl.BlockSpec(memory_space=pltpu.SMEM)
    vmem = pl.BlockSpec(memory_space=pltpu.VMEM)
    hbm = pl.BlockSpec(memory_space=pltpu.HBM)
    return pl.pallas_call(
        cut_kernel,
        out_shape=(
            jax.ShapeDtypeStruct((8, 512, 128), BF),
            jax.ShapeDtypeStruct((512, 128), BF),
            jax.ShapeDtypeStruct((512, 128), F32),
        ),
        in_specs=[smem, vmem, vmem, vmem, hbm, hbm],
        out_specs=(vmem, vmem, vmem),
        scratch_shapes=[
            pltpu.VMEM((2, WIN + 16, 128), BF),
            pltpu.VMEM((2, WIN + 16, 128), BF),
            pltpu.VMEM((2, WIN + 16, 128), F32),
            pltpu.SemaphoreType.DMA((2, 2)),
        ],
        compiler_params=pltpu.CompilerParams(vmem_limit_bytes=60 * 2**20),
        name="cut_windows",
    )(
        position.reshape(1),
        slot_source.reshape(1, 128),
        episode_pick.reshape(1, 128),
        window_start.reshape(1, 128),
        latents,
        labels,
    )


def three_parts(x):
    high = lax.reduce_precision(x, 8, 7)
    rest = x - high
    mid = lax.reduce_precision(rest, 8, 7)
    return jnp.concatenate([high, mid, rest - mid]).astype(BF)


def on_device(
    latents, labels, slot_source, episode_pick, window_start, proj_weight, norm_gain, head_weight
):
    position = lax.axis_index("dp")
    c, xl, zl, zh = position % 2, (position // 2) % 2, (position // 4) % 4, position // 16
    own_copies, own, targets = cut_windows(
        latents, labels, slot_source, episode_pick, window_start, position
    )

    pieces = exchange(
        jnp.transpose(own.reshape(2, 64, 4, 128), (1, 0, 2, 3)).reshape(128, 4, 128), "dp"
    )
    proj = gather(proj_weight, "dp", Z_GROUPS).reshape(16, 16, 768)
    proj, pieces = tie(proj, pieces)
    own_copies, pieces = tie(own_copies, pieces)

    gathered = exchange(own_copies, "mp")
    proj = pair(proj, permute(proj, to_xlo), xl)
    proj = pair(proj, permute(proj, to_core), c)
    proj = jnp.transpose(proj, (2, 1, 0, 3, 4)).reshape(1024, 768)
    ordered, gathered = tie(pieces[slot_source], gathered)
    arrived = exchange(ordered, "dp")
    inputs = jnp.transpose(gathered, (1, 0, 2)).reshape(512, 1024)

    hidden = jnp.dot(inputs, proj, preferred_element_type=F32)
    local_mean = jnp.sum(hidden, axis=1) / 768
    centred = hidden - local_mean[:, None]
    square = jnp.sum(centred * centred, axis=1)
    scaled = (centred * norm_gain).astype(BF)
    partial = jnp.dot(scaled, head_weight, preferred_element_type=F32).astype(BF)
    gain_head = jnp.sum(norm_gain[:, None] * head_weight.astype(F32), axis=0)
    sums = jnp.concatenate(
        [local_mean.reshape(4, 128), square.reshape(4, 128), gain_head[None]], axis=0
    )
    sent = jnp.concatenate([partial, three_parts(sums), jnp.zeros((101, 128), BF)], axis=0)
    sent, arrived = tie(copies(sent, 8), arrived)
    all_sent = exchange(sent, "mp")
    arrived = jnp.transpose(arrived.reshape(64, 2, 4, 128), (1, 0, 2, 3)).reshape(512, 128)
    arrived, all_sent = tie(copies(arrived, 8), all_sent)
    there = exchange(arrived, "mp")
    summed = jnp.sum(all_sent[:, :512].astype(F32), axis=0)
    sums = jnp.sum(all_sent[:, 512:539].astype(F32).reshape(8, 3, 9, 128), axis=1)
    means = sums[:, :4].reshape(8, 512)
    squares = sums[:, 4:8].reshape(8, 512)
    gain_heads = sums[:, 8]

    def statistics(means, squares):
        mean = jnp.sum(means, axis=0) / 8
        off = means - mean
        variance = (jnp.sum(squares, axis=0) + 768 * jnp.sum(off * off, axis=0)) / D
        return mean, off, lax.rsqrt(variance + EPSILON)

    row_mean, off, row_scale = statistics(means, squares)
    shift = sum(off[m][:, None] * gain_heads[m][None, :] for m in range(8))
    predicted = row_scale[:, None] * (summed + shift)
    error_grad = ((predicted - targets) / math.sqrt(32768)).astype(BF)
    error_wide = error_grad.astype(F32)
    normed = (hidden - row_mean[:, None]) * row_scale[:, None]
    features_here = (normed * norm_gain).astype(BF)
    head_term = lax.dot_general(
        error_grad, features_here, (((0,), (0,)), ((), ())), preferred_element_type=F32
    )
    back_feat = lax.dot_general(
        error_grad, head_weight, (((1,), (1,)), ((), ())), preferred_element_type=F32
    )
    gain_term = jnp.sum(back_feat * normed, axis=0)
    first_sum = jnp.sum(error_wide * jnp.sum(gain_heads, axis=0), axis=1)
    second_sum = jnp.sum(error_wide * predicted, axis=1)
    back_hidden = (
        row_scale[:, None]
        * (
            back_feat * norm_gain
            - first_sum[:, None] / D
            - normed * (second_sum[:, None] / D)
        )
    ).astype(BF)
    full_term = lax.dot_general(
        inputs, back_hidden, (((0,), (0,)), ((), ())), preferred_element_type=F32
    )

    gain_rows = jnp.pad(gain_term.reshape(16, 1, 48), ((0, 0), (0, 7), (0, 80)))
    head_rows = jnp.concatenate([head_term.reshape(16, 8, 768), gain_rows], axis=2).astype(BF)
    head_rows, there = tie(head_rows, there)
    part = exchange(head_rows, "dp", Z_GROUPS)
    blocks = full_term.reshape(16, 2, 2, 16, 768)
    kept = take(blocks, c, 2) + permute(take(blocks, 1 - c, 2), to_core)
    part, kept = tie(part, kept)

    inputs_there = jnp.transpose(there, (1, 0, 2)).reshape(512, 1024)
    hidden_there = jnp.dot(inputs_there, proj, preferred_element_type=F32)
    local_mean = jnp.sum(hidden_there, axis=1) / 768
    centred = hidden_there - local_mean[:, None]
    square = jnp.sum(centred * centred, axis=1)
    sums = jnp.concatenate([local_mean.reshape(4, 128), square.reshape(4, 128)], axis=0)
    sums, part = tie(copies(sums, 8), part)
    sums = exchange(sums, "mp")

    part = jnp.sum(part.astype(F32), axis=0)
    part = part + permute(part, to_core)
    kept = take(kept, xl, 1) + permute(take(kept, 1 - xl, 1).astype(BF), to_xlo).astype(F32)
    part, kept = tie(part, kept)
    part = part + permute(part, to_xlo)
    kept = scatter4(jnp.transpose(kept.reshape(4, 4, 16, 768), (1, 0, 2, 3)), zl, to_zl)
    part, kept = tie(part, kept)
    part, sums = tie(copies(part.astype(BF), 16), sums)
    whole = exchange(part, "dp", Z_GROUPS).astype(F32)
    grad_head = jnp.transpose(whole[:, :, :768].reshape(128, 768))
    grad_gain = whole[:, 0, 768:816].reshape(768)
    grad_proj = scatter4(kept, zh, to_zh)

    mean, _, scale = statistics(sums[:, :4].reshape(8, 512), sums[:, 4:].reshape(8, 512))
    features = (((hidden_there - mean[:, None]) * scale[:, None]) * norm_gain).astype(BF)
    return (grad_proj, grad_head, grad_gain, features)


def solution(mesh):
    in_specs = (
        P("dp", None, "mp"),
        P("dp", None, None),
        P(),
        P(),
        P(),
        P("dp", "mp"),
        P("mp"),
        P("mp", None),
    )
    out_specs = (P("dp", "mp"), P("mp", None), P("mp"), P("dp", "mp"))
    return jax.shard_map(
        on_device, mesh=mesh, in_specs=in_specs, out_specs=out_specs, check_vma=False
    )
```

time: 1090 us -> 267 us (0.24)
  the two profiles are of different devices: /device:TPU:8 before, /device:TPU:4 now
where the time goes in v1:
time: 267 us; the launch traced here: 265 us
  starting transfers between devices  111 us (42%)
  waiting for transfers between devices  79.2 us (30%)
  blocking collectives  34.1 us (13%)
  local copies, waits for them, and re-layouts  16 us (6%)
  other arithmetic  13.9 us (5%)
  matrix products  6.29 us (2%)
  Pallas kernels  2.98 us (1%)
    all_to_all x8, waiting for transfers between devices, exchange(): lax.all_to_all(x, axis, split_axis=0, concat_axis=0, tiled=True, axis_ind...  75.5 us
    all_to_all x8, starting transfers between devices, exchange(): lax.all_to_all(x, axis, split_axis=0, concat_axis=0, tiled=True, axis_ind...  69 us
    ppermute x12, starting transfers between devices, permute(): return lax.ppermute(x, 'dp', [(i, target(i)) for i in range(N_DP)])  42.5 us
    all_gather x1, blocking collectives, gather(): return lax.all_gather(x, axis, axis=0, tiled=True, axis_index_groups=groups)  34.1 us
  transfers between devices with their start and end apart: 20, of which 8 were waited for; matrix products, arithmetic and copies ran while one was open for 8% of the time, Pallas kernels for 0%

profile of v1, /device:TPU:4, one launch (start us, length us, event | category | flops | bytes accessed | tf_op | source)
XLA Modules:
  0.0 265.3 jit_solution(6132149909210616649)
XLA Ops:
  0.6 3.0 %cut_windows.1 = (bf16[8,512,128]{2,1,0:T(8,128)(2,1)}, bf16[512,128]{1,0:T(8,128)(2,1)}, f32[512,128]{1,0:T(8,128)}) custom-call(s32[1]{0:T(128)} %bitcast.position_ref, s32[1,128]{1,0:T(1,128)} %bitcast.164, s32[1,128]{1,0:T(1,128)} %bitcast.162, s32[1,128]{1,0:T(1,128)} %bitcast.163, bf16[8,512,128]{2,1,0:T(8,128)(2,1)} %latents_ref.1, ...), custom_call_target="tpu_custom_call" | custom-call | tf_op jit(solution)/shard_map/cut_windows/pallas_call | solution.py:109
  3.6 1.0 copy.57
  5.4 16.7 %all-to-all-start = ((bf16[128,4,128]{2,1,0:T(4,128)(2,1)}), bf16[128,4,128]{2,1,0:T(4,128)(2,1)S(1)}, u32[]{:S(2)}, u32[]{:S(2)}) async-start(bf16[128,4,128]{2,1,0:T(4,128)(2,1)} %copy.58), calls=%async_computation | async-start | bytes 262144 | tf_op jit(solution)/shard_map/all_to_all | solution.py:41
  22.2 34.1 %all_gather.3 = bf16[256,768]{1,0:T(8,128)(2,1)S(1)} all-gather(bf16[16,768]{1,0:T(8,128)(2,1)S(1)} %copy-done.11), channel_id=1, replica_groups={{0,32,64,96,128,160,192,224,256,288,320,352,384,416,448,480},{8,40,72,1..., dimensions={0}, use_global_device_ids=true | all-gather | bytes 417792 | tf_op jit(solution)/shard_map/all_gather | solution.py:47
  56.3 3.3 %collective-permute-start = (bf16[16,16,768]{2,1,0:T(8,128)(2,1)S(1)}, bf16[16,16,768]{2,1,0:T(8,128)(2,1)S(1)}, u32[]{:S(2)}, u32[]{:S(2)}) collective-permute-start(bf16[16,16,768]{2,1,0:T(8,128)(2,1)S(1)} %bitcast.137), channel_id=1, source_target_pairs={{0,16},{8,24},{16,0},{24,8},{32,48},{40,56},{48,32},{56,40},{64,80... | collective-permute-start | bytes 1179656 | tf_op jit(solution)/shard_map/ppermute | solution.py:37
  59.7 7.6 %all-to-all-start.1 = ((bf16[8,512,128]{2,1,0:T(8,128)(2,1)}), bf16[8,512,128]{2,1,0:T(8,128)(2,1)S(1)}, u32[]{:S(2)}, u32[]{:S(2)}) async-start(bf16[8,512,128]{2,1,0:T(8,128)(2,1)} %get-tuple-element.33), calls=%async_computation.1 | async-start | bytes 2097152 | tf_op jit(solution)/shard_map/all_to_all | solution.py:41
  67.2 2.3 collective-permute-done
  69.5 1.0 maximum_select_fusion.1
  70.4 1.9 collective-permute-start.1
  72.6 1.4 gather_fusion
  74.2 4.4 %all-to-all-done.1 = bf16[8,512,128]{2,1,0:T(8,128)(2,1)S(1)} async-done(((bf16[8,512,128]{2,1,0:T(8,128)(2,1)}), bf16[8,512,128]{2,1,0:T(8,128)(2,1)S(1)}, u32[]{:S(2)}, u32[]{:S(2)}) %all-to-all-start.1) | async-done | bytes 1048608 | tf_op jit(solution)/shard_map/all_to_all | solution.py:41
  79.1 11.0 %all-to-all-start.2 = ((bf16[128,4,128]{2,1,0:T(4,128)(2,1)}), bf16[128,4,128]{2,1,0:T(4,128)(2,1)S(1)}, u32[]{:S(2)}, u32[]{:S(2)}) async-start(bf16[128,4,128]{2,1,0:T(4,128)(2,1)} %gather_fusion), calls=%async_computation.2 | async-start | bytes 262144 | tf_op jit(solution)/shard_map/all_to_all | solution.py:41
  90.2 1.6 maximum_select_fusion
  91.8 1.1 fusion.35
  94.8 12.4 %all-to-all-done.2 = bf16[128,4,128]{2,1,0:T(4,128)(2,1)S(1)} async-done(((bf16[128,4,128]{2,1,0:T(4,128)(2,1)}), bf16[128,4,128]{2,1,0:T(4,128)(2,1)S(1)}, u32[]{:S(2)}, u32[]{:S(2)}) %all-to-all-start.2) | async-done | bytes 131104 | tf_op jit(solution)/shard_map/all_to_all | solution.py:41
  107.2 1.2 broadcast_in_dim.19
  108.4 7.5 %all-to-all-start.3 = ((bf16[8,640,128]{2,1,0:T(8,128)(2,1)}), bf16[8,640,128]{2,1,0:T(8,128)(2,1)S(1)}, u32[]{:S(2)}, u32[]{:S(2)}) async-start(bf16[8,640,128]{2,1,0:T(8,128)(2,1)} %broadcast_in_dim.19), calls=%async_computation.3 | async-start | bytes 2621440 | tf_op jit(solution)/shard_map/all_to_all | solution.py:41
  116.1 17.8 %all-to-all-done.3 = bf16[8,640,128]{2,1,0:T(8,128)(2,1)S(1)} async-done(((bf16[8,640,128]{2,1,0:T(8,128)(2,1)}), bf16[8,640,128]{2,1,0:T(8,128)(2,1)S(1)}, u32[]{:S(2)}, u32[]{:S(2)}) %all-to-all-start.3) | async-done | bytes 1310752 | tf_op jit(solution)/shard_map/all_to_all | solution.py:41
  133.9 1.2 broadcast_in_dim.21
  136.2 1.0 fusion.16
  138.5 1.4 fusion.2
  139.9 1.4 dynamic-slice_bitcast_fusion
  142.0 1.9 collective-permute-start.2
  144.0 6.9 %all-to-all-start.4 = ((bf16[8,512,128]{1,2,0:T(8,128)(2,1)}), bf16[8,512,128]{1,2,0:T(8,128)(2,1)}, u32[]{:S(2)}, u32[]{:S(2)}) async-start(bf16[8,512,128]{1,2,0:T(8,128)(2,1)} %broadcast_in_dim.21), calls=%async_computation.4 | async-start | bytes 2097152 | tf_op jit(solution)/shard_map/all_to_all | solution.py:41
  152.1 14.3 %all-to-all-done.4 = bf16[8,512,128]{1,2,0:T(8,128)(2,1)} async-done(((bf16[8,512,128]{1,2,0:T(8,128)(2,1)}), bf16[8,512,128]{1,2,0:T(8,128)(2,1)}, u32[]{:S(2)}, u32[]{:S(2)}) %all-to-all-start.4) | async-done | bytes 1048608 | tf_op jit(solution)/shard_map/all_to_all | solution.py:41
  166.4 4.4 %all-to-all-start.5 = ((bf16[16,8,896]{2,1,0:T(8,128)(2,1)}), bf16[16,8,896]{2,1,0:T(8,128)(2,1)}, u32[]{:S(2)}, u32[]{:S(2)}) async-start(bf16[16,8,896]{2,1,0:T(8,128)(2,1)} %fusion.18), calls=%async_computation.5 | async-start | bytes 458752 | tf_op jit(solution)/shard_map/all_to_all | solution.py:41
  170.8 2.5 fusion.36
  173.3 1.7 bitcast_add_fusion
  175.0 12.5 %all-to-all-done.5 = bf16[16,8,896]{2,1,0:T(8,128)(2,1)} async-done(((bf16[16,8,896]{2,1,0:T(8,128)(2,1)}), bf16[16,8,896]{2,1,0:T(8,128)(2,1)}, u32[]{:S(2)}, u32[]{:S(2)}) %all-to-all-start.5) | async-done | bytes 229408 | tf_op jit(solution)/shard_map/all_to_all | solution.py:41
  188.3 2.7 %collective-permute-start.4 = (bf16[16,16,768]{2,1,0:T(8,128)(2,1)}, bf16[16,16,768]{2,1,0:T(8,128)(2,1)S(1)}, u32[]{:S(2)}, u32[]{:S(2)}) collective-permute-start(bf16[16,16,768]{2,1,0:T(8,128)(2,1)} %fusion.15), channel_id=1, source_target_pairs={{0,16},{8,24},{16,0},{24,8},{32,48},{40,56},{48,32},{56,40},{64,80... | collective-permute-start | bytes 1179656 | tf_op jit(solution)/shard_map/ppermute | solution.py:37
  192.0 1.6 convert_reduce_fusion.1
  193.5 1.9 collective-permute-start.3
  195.6 1.4 collective-permute-done.3
  197.0 1.4 add.207
  198.5 0.9 copy-done.4
  199.4 7.4 %collective-permute-start.8 = (bf16[4,16,768]{2,1,0:T(8,128)(2,1)S(1)}, bf16[4,16,768]{2,1,0:T(8,128)(2,1)S(1)}, u32[]{:S(2)}, u32[]{:S(2)}) collective-permute-start(bf16[4,16,768]{2,1,0:T(8,128)(2,1)S(1)} %get-tuple-element.82), channel_id=1, source_target_pairs={{0,96},{8,104},{16,112},{24,120},{32,0},{40,8},{48,16},{56,24},{64... | collective-permute-start | bytes 294920 | tf_op jit(solution)/shard_map/ppermute | solution.py:37
  206.8 2.6 collective-permute-start.7
  209.4 1.9 collective-permute-start.6
  211.3 2.7 %collective-permute-start.5 = (f32[8,896]{1,0:T(8,128)}, f32[8,896]{1,0:T(8,128)S(1)}, u32[]{:S(2)}, u32[]{:S(2)}) collective-permute-start(f32[8,896]{1,0:T(8,128)} %add.207), channel_id=1, source_target_pairs={{0,16},{8,24},{16,0},{24,8},{32,48},{40,56},{48,32},{56,40},{64,80... | collective-permute-start | bytes 86024 | tf_op jit(solution)/shard_map/ppermute | solution.py:37
  214.1 6.0 %all-to-all-start.6 = ((f32[8,8,128]{2,1,0:T(8,128)}), f32[8,8,128]{2,1,0:T(8,128)S(1)}, u32[]{:S(2)}, u32[]{:S(2)}) async-start(f32[8,8,128]{2,1,0:T(8,128)} %broadcast_in_dim.22), calls=%async_computation.6 | async-start | bytes 65536 | tf_op jit(solution)/shard_map/all_to_all | solution.py:41
  220.9 1.0 fusion.20
  221.9 5.6 %collective-permute-start.11 = (bf16[16,768]{1,0:T(8,128)(2,1)S(1)}, bf16[16,768]{1,0:T(8,128)(2,1)S(1)}, u32[]{:S(2)}, u32[]{:S(2)}) collective-permute-start(bf16[16,768]{1,0:T(8,128)(2,1)S(1)} %get-tuple-element.87), channel_id=1, source_target_pairs={{0,384},{8,392},{16,400},{24,408},{32,416},{40,424},{48,432},{56,4... | collective-permute-start | bytes 73736 | tf_op jit(solution)/shard_map/ppermute | solution.py:37
  227.6 6.5 %collective-permute-start.10 = (bf16[16,768]{1,0:T(8,128)(2,1)S(1)}, bf16[16,768]{1,0:T(8,128)(2,1)S(1)}, u32[]{:S(2)}, u32[]{:S(2)}) collective-permute-start(bf16[16,768]{1,0:T(8,128)(2,1)S(1)} %get-tuple-element.88), channel_id=1, source_target_pairs={{0,256},{8,264},{16,272},{24,280},{32,288},{40,296},{48,304},{56,3... | collective-permute-start | bytes 73736 | tf_op jit(solution)/shard_map/ppermute | solution.py:37
  234.0 4.0 %collective-permute-start.9 = (bf16[16,768]{1,0:T(8,128)(2,1)S(1)}, bf16[16,768]{1,0:T(8,128)(2,1)S(1)}, u32[]{:S(2)}, u32[]{:S(2)}) collective-permute-start(bf16[16,768]{1,0:T(8,128)(2,1)S(1)} %get-tuple-element.86), channel_id=1, source_target_pairs={{0,128},{8,136},{16,144},{24,152},{32,160},{40,168},{48,176},{56,1... | collective-permute-start | bytes 73736 | tf_op jit(solution)/shard_map/ppermute | solution.py:37
  238.8 8.9 %all-to-all-start.7 = ((bf16[16,8,896]{2,1,0:T(8,128)(2,1)}), bf16[16,8,896]{2,1,0:T(8,128)(2,1)S(1)}, u32[]{:S(2)}, u32[]{:S(2)}) async-start(bf16[16,8,896]{2,1,0:T(8,128)(2,1)} %broadcast_in_dim.23), calls=%async_computation.7 | async-start | bytes 458752 | tf_op jit(solution)/shard_map/all_to_all | solution.py:41
  247.7 1.1 multiply_convert_fusion
  249.5 14.1 %all-to-all-done.7 = bf16[16,8,896]{2,1,0:T(8,128)(2,1)S(1)} async-done(((bf16[16,8,896]{2,1,0:T(8,128)(2,1)}), bf16[16,8,896]{2,1,0:T(8,128)(2,1)S(1)}, u32[]{:S(2)}, u32[]{:S(2)}) %all-to-all-start.7) | async-done | bytes 229408 | tf_op jit(solution)/shard_map/all_to_all | solution.py:41
  263.7 0.9 copy.71
  (88 shorter events, 12.9 us)
Async XLA Ops:
  0.6 21.5 %copy-start.11 = (bf16[16,768]{1,0:T(8,128)(2,1)S(1)}, bf16[16,768]{1,0:T(8,128)(2,1)}, u32[]{:S(2)}) copy-start(bf16[16,768]{1,0:T(8,128)(2,1)} %param.13) | copy-start | bytes 73732
  5.4 50.9 %all-to-all-start = ((bf16[128,4,128]{2,1,0:T(4,128)(2,1)}), bf16[128,4,128]{2,1,0:T(4,128)(2,1)S(1)}, u32[]{:S(2)}, u32[]{:S(2)}) async-start(bf16[128,4,128]{2,1,0:T(4,128)(2,1)} %copy.58), calls=%async_computation | async-start | bytes 262144 | tf_op jit(solution)/shard_map/all_to_all | solution.py:41
  56.3 13.2 %collective-permute-start = (bf16[16,16,768]{2,1,0:T(8,128)(2,1)S(1)}, bf16[16,16,768]{2,1,0:T(8,128)(2,1)S(1)}, u32[]{:S(2)}, u32[]{:S(2)}) collective-permute-start(bf16[16,16,768]{2,1,0:T(8,128)(2,1)S(1)} %bitcast.137), channel_id=1, source_target_pairs={{0,16},{8,24},{16,0},{24,8},{32,48},{40,56},{48,32},{56,40},{64,80... | collective-permute-start | bytes 1179656 | tf_op jit(solution)/shard_map/ppermute | solution.py:37
  59.6 12.7 %copy-start.12 = (s32[128]{0:T(128)S(1)}, s32[128]{0:T(128)}, u32[]{:S(2)}) copy-start(s32[128]{0:T(128)} %param.10) | copy-start | bytes 1540
  59.6 12.8 %copy-start.5 = (bf16[768,128]{1,0:T(8,128)(2,1)S(1)}, bf16[768,128]{1,0:T(8,128)(2,1)}, u32[]{:S(2)}) copy-start(bf16[768,128]{1,0:T(8,128)(2,1)} %param.15) | copy-start | bytes 589828
  59.6 12.8 %copy-start.10 = (f32[768]{0:T(1024)S(1)}, f32[768]{0:T(1024)}, u32[]{:S(2)}) copy-start(f32[768]{0:T(1024)} %param.14) | copy-start | bytes 9220
  59.7 18.9 %all-to-all-start.1 = ((bf16[8,512,128]{2,1,0:T(8,128)(2,1)}), bf16[8,512,128]{2,1,0:T(8,128)(2,1)S(1)}, u32[]{:S(2)}, u32[]{:S(2)}) async-start(bf16[8,512,128]{2,1,0:T(8,128)(2,1)} %get-tuple-element.33), calls=%async_computation.1 | async-start | bytes 2097152 | tf_op jit(solution)/shard_map/all_to_all | solution.py:41
  70.4 19.7 %collective-permute-start.1 = (bf16[2,16,16,768]{3,2,0,1:T(8,128)(2,1)}, bf16[2,16,16,768]{3,2,0,1:T(8,128)(2,1)}, u32[]{:S(2)}, u32[]{:S(2)}) collective-permute-start(bf16[2,16,16,768]{3,2,0,1:T(8,128)(2,1)} %maximum_select_fusion.1), channel_id=1, source_target_pairs={{0,8},{8,0},{16,24},{24,16},{32,40},{40,32},{48,56},{56,48},{64,72... | collective-permute-start | bytes 2359304 | tf_op jit(solution)/shard_map/ppermute | solution.py:37
  79.1 12.7 %copy-start.2 = (bf16[512,8,128]{0,2,1:T(8,128)(2,1)}, bf16[512,8,128]{0,2,1:T(8,128)(2,1)S(1)}, u32[]{:S(2)}) copy-start(bf16[512,8,128]{0,2,1:T(8,128)(2,1)S(1)} %copy.59) | copy-start | bytes 3145732
  79.1 28.1 %all-to-all-start.2 = ((bf16[128,4,128]{2,1,0:T(4,128)(2,1)}), bf16[128,4,128]{2,1,0:T(4,128)(2,1)S(1)}, u32[]{:S(2)}, u32[]{:S(2)}) async-start(bf16[128,4,128]{2,1,0:T(4,128)(2,1)} %gather_fusion), calls=%async_computation.2 | async-start | bytes 262144 | tf_op jit(solution)/shard_map/all_to_all | solution.py:41
  91.8 1.2 copy-start.7
  92.9 0.9 copy-start.6
  108.4 25.5 %all-to-all-start.3 = ((bf16[8,640,128]{2,1,0:T(8,128)(2,1)}), bf16[8,640,128]{2,1,0:T(8,128)(2,1)S(1)}, u32[]{:S(2)}, u32[]{:S(2)}) async-start(bf16[8,640,128]{2,1,0:T(8,128)(2,1)} %broadcast_in_dim.19), calls=%async_computation.3 | async-start | bytes 2621440 | tf_op jit(solution)/shard_map/all_to_all | solution.py:41
  135.1 1.2 copy-start.9
  137.3 1.2 copy-start.3
  139.9 2.1 copy-start
  142.0 31.3 %collective-permute-start.2 = (f32[16,2,16,768]{3,2,1,0:T(8,128)}, f32[16,2,16,768]{3,2,1,0:T(8,128)}, u32[]{:S(2)}, u32[]{:S(2)}) collective-permute-start(f32[16,2,16,768]{3,2,1,0:T(8,128)} %dynamic-slice_bitcast_fusion), channel_id=1, source_target_pairs={{0,8},{8,0},{16,24},{24,16},{32,40},{40,32},{48,56},{56,48},{64,72... | collective-permute-start | bytes 4718600 | tf_op jit(solution)/shard_map/ppermute | solution.py:37
  144.0 22.5 %all-to-all-start.4 = ((bf16[8,512,128]{1,2,0:T(8,128)(2,1)}), bf16[8,512,128]{1,2,0:T(8,128)(2,1)}, u32[]{:S(2)}, u32[]{:S(2)}) async-start(bf16[8,512,128]{1,2,0:T(8,128)(2,1)} %broadcast_in_dim.21), calls=%async_computation.4 | async-start | bytes 2097152 | tf_op jit(solution)/shard_map/all_to_all | solution.py:41
  150.8 20.0 %copy-start.8 = (bf16[2,2,16,16,768]{4,3,0,1,2:T(8,128)(2,1)S(1)}, bf16[2,2,16,16,768]{4,3,0,1,2:T(8,128)(2,1)}, u32[]{:S(2)}) copy-start(bf16[2,2,16,16,768]{4,3,0,1,2:T(8,128)(2,1)} %copy-done.7) | copy-start | bytes 4718596
  166.4 21.1 %all-to-all-start.5 = ((bf16[16,8,896]{2,1,0:T(8,128)(2,1)}), bf16[16,8,896]{2,1,0:T(8,128)(2,1)}, u32[]{:S(2)}, u32[]{:S(2)}) async-start(bf16[16,8,896]{2,1,0:T(8,128)(2,1)} %fusion.18), calls=%async_computation.5 | async-start | bytes 458752 | tf_op jit(solution)/shard_map/all_to_all | solution.py:41
  170.8 2.5 copy-start.1
  188.3 10.0 %collective-permute-start.4 = (bf16[16,16,768]{2,1,0:T(8,128)(2,1)}, bf16[16,16,768]{2,1,0:T(8,128)(2,1)S(1)}, u32[]{:S(2)}, u32[]{:S(2)}) collective-permute-start(bf16[16,16,768]{2,1,0:T(8,128)(2,1)} %fusion.15), channel_id=1, source_target_pairs={{0,16},{8,24},{16,0},{24,8},{32,48},{40,56},{48,32},{56,40},{64,80... | collective-permute-start | bytes 1179656 | tf_op jit(solution)/shard_map/ppermute | solution.py:37
  193.5 3.4 %collective-permute-start.3 = (f32[8,896]{1,0:T(8,128)}, f32[8,896]{1,0:T(8,128)}, u32[]{:S(2)}, u32[]{:S(2)}) collective-permute-start(f32[8,896]{1,0:T(8,128)} %convert_reduce_fusion.1), channel_id=1, source_target_pairs={{0,8},{8,0},{16,24},{24,16},{32,40},{40,32},{48,56},{56,48},{64,72... | collective-permute-start | bytes 86024 | tf_op jit(solution)/shard_map/ppermute | solution.py:37
  198.4 0.9 copy-start.4
  199.4 21.5 %collective-permute-start.8 = (bf16[4,16,768]{2,1,0:T(8,128)(2,1)S(1)}, bf16[4,16,768]{2,1,0:T(8,128)(2,1)S(1)}, u32[]{:S(2)}, u32[]{:S(2)}) collective-permute-start(bf16[4,16,768]{2,1,0:T(8,128)(2,1)S(1)} %get-tuple-element.82), channel_id=1, source_target_pairs={{0,96},{8,104},{16,112},{24,120},{32,0},{40,8},{48,16},{56,24},{64... | collective-permute-start | bytes 294920 | tf_op jit(solution)/shard_map/ppermute | solution.py:37
  206.8 14.2 %collective-permute-start.7 = (bf16[4,16,768]{2,1,0:T(8,128)(2,1)S(1)}, bf16[4,16,768]{2,1,0:T(8,128)(2,1)S(1)}, u32[]{:S(2)}, u32[]{:S(2)}) collective-permute-start(bf16[4,16,768]{2,1,0:T(8,128)(2,1)S(1)} %get-tuple-element.83), channel_id=1, source_target_pairs={{0,64},{8,72},{16,80},{24,88},{32,96},{40,104},{48,112},{56,120},{... | collective-permute-start | bytes 294920 | tf_op jit(solution)/shard_map/ppermute | solution.py:37
  209.4 11.5 %collective-permute-start.6 = (bf16[4,16,768]{2,1,0:T(8,128)(2,1)S(1)}, bf16[4,16,768]{2,1,0:T(8,128)(2,1)S(1)}, u32[]{:S(2)}, u32[]{:S(2)}) collective-permute-start(bf16[4,16,768]{2,1,0:T(8,128)(2,1)S(1)} %get-tuple-element.81), channel_id=1, source_target_pairs={{0,32},{8,40},{16,48},{24,56},{32,64},{40,72},{48,80},{56,88},{64,... | collective-permute-start | bytes 294920 | tf_op jit(solution)/shard_map/ppermute | solution.py:37
  211.3 8.8 %collective-permute-start.5 = (f32[8,896]{1,0:T(8,128)}, f32[8,896]{1,0:T(8,128)S(1)}, u32[]{:S(2)}, u32[]{:S(2)}) collective-permute-start(f32[8,896]{1,0:T(8,128)} %add.207), channel_id=1, source_target_pairs={{0,16},{8,24},{16,0},{24,8},{32,48},{40,56},{48,32},{56,40},{64,80... | collective-permute-start | bytes 86024 | tf_op jit(solution)/shard_map/ppermute | solution.py:37
  214.1 23.9 %all-to-all-start.6 = ((f32[8,8,128]{2,1,0:T(8,128)}), f32[8,8,128]{2,1,0:T(8,128)S(1)}, u32[]{:S(2)}, u32[]{:S(2)}) async-start(f32[8,8,128]{2,1,0:T(8,128)} %broadcast_in_dim.22), calls=%async_computation.6 | async-start | bytes 65536 | tf_op jit(solution)/shard_map/all_to_all | solution.py:41
  221.9 26.9 %collective-permute-start.11 = (bf16[16,768]{1,0:T(8,128)(2,1)S(1)}, bf16[16,768]{1,0:T(8,128)(2,1)S(1)}, u32[]{:S(2)}, u32[]{:S(2)}) collective-permute-start(bf16[16,768]{1,0:T(8,128)(2,1)S(1)} %get-tuple-element.87), channel_id=1, source_target_pairs={{0,384},{8,392},{16,400},{24,408},{32,416},{40,424},{48,432},{56,4... | collective-permute-start | bytes 73736 | tf_op jit(solution)/shard_map/ppermute | solution.py:37
  227.6 21.3 %collective-permute-start.10 = (bf16[16,768]{1,0:T(8,128)(2,1)S(1)}, bf16[16,768]{1,0:T(8,128)(2,1)S(1)}, u32[]{:S(2)}, u32[]{:S(2)}) collective-permute-start(bf16[16,768]{1,0:T(8,128)(2,1)S(1)} %get-tuple-element.88), channel_id=1, source_target_pairs={{0,256},{8,264},{16,272},{24,280},{32,288},{40,296},{48,304},{56,3... | collective-permute-start | bytes 73736 | tf_op jit(solution)/shard_map/ppermute | solution.py:37
  234.0 14.8 %collective-permute-start.9 = (bf16[16,768]{1,0:T(8,128)(2,1)S(1)}, bf16[16,768]{1,0:T(8,128)(2,1)S(1)}, u32[]{:S(2)}, u32[]{:S(2)}) collective-permute-start(bf16[16,768]{1,0:T(8,128)(2,1)S(1)} %get-tuple-element.86), channel_id=1, source_target_pairs={{0,128},{8,136},{16,144},{24,152},{32,160},{40,168},{48,176},{56,1... | collective-permute-start | bytes 73736 | tf_op jit(solution)/shard_map/ppermute | solution.py:37
  238.8 24.9 %all-to-all-start.7 = ((bf16[16,8,896]{2,1,0:T(8,128)(2,1)}), bf16[16,8,896]{2,1,0:T(8,128)(2,1)S(1)}, u32[]{:S(2)}, u32[]{:S(2)}) async-start(bf16[16,8,896]{2,1,0:T(8,128)(2,1)} %broadcast_in_dim.23), calls=%async_computation.7 | async-start | bytes 458752 | tf_op jit(solution)/shard_map/all_to_all | solution.py:41

commit v2 on v1

v2 whole, which is shorter than its diff:
```python
import math

import jax
import jax.numpy as jnp
from jax import lax
from jax.experimental import pallas as pl
from jax.experimental.pallas import tpu as pltpu
from jax.sharding import PartitionSpec as P

D = 6144
WIN = 256
EPSILON = 1e-05
BF = jnp.bfloat16
F32 = jnp.float32

N_DP = 64
Z_GROUPS = [[z * 4 + q for z in range(16)] for q in range(4)]
ZH_GROUPS = [[zh * 16 + q for zh in range(4)] for q in range(16)]
ZL_GROUPS = [[zh * 16 + zl * 4 + q for zl in range(4)] for zh in range(4) for q in range(4)]


def to_core(i):
    return i ^ 1


def to_xlo(i):
    return i ^ 2


def to_zl(k):
    return lambda i: (i & ~12) | ((i + 4 * k) & 12)


def to_zh(k):
    return lambda i: (i + 16 * k) % N_DP


def permute(x, target):
    return lax.ppermute(x, "dp", [(i, target(i)) for i in range(N_DP)])


def exchange(x, axis, groups=None):
    return lax.all_to_all(
        x, axis, split_axis=0, concat_axis=0, tiled=True, axis_index_groups=groups
    )


def gather(x, axis, groups=None):
    return lax.all_gather(x, axis, axis=0, tiled=True, axis_index_groups=groups)


def copies(x, n):
    return jnp.broadcast_to(x[None], (n,) + x.shape)


def take(x, index, axis):
    return lax.dynamic_index_in_dim(x, index, axis, keepdims=False)


def pair(mine, other, index):
    return jnp.where(index == 0, jnp.stack([mine, other]), jnp.stack([other, mine]))


def scatter4(blocks, index, to):
    total = take(blocks, index, 0)
    for k in (1, 2, 3):
        sent = take(blocks, (index + k) % 4, 0).astype(BF)
        total = total + permute(sent, to(k)).astype(F32)
    return total


def tie(x, y):
    return lax.optimization_barrier((x, y))


PEERS = 64


def cut_kernel(
    position_ref, slot_ref, pick_ref, start_ref, latents_ref, labels_ref,
    pieces_ref, lat_held, lab_held, wide, sems,
):
    shifts, moves = [], []
    for k in range(2):
        here = slot_ref[...] == position_ref[0] * 2 + k
        episode = jnp.sum(jnp.where(here, pick_ref[...], 0).astype(F32)).astype(jnp.int32)
        start = jnp.sum(jnp.where(here, start_ref[...], 0).astype(F32)).astype(jnp.int32)
        first = pl.multiple_of(jnp.minimum(start // 16, 15) * 16, 16)
        shifts.append(start - first)
        for n, (store, held) in enumerate(((latents_ref, lat_held), (labels_ref, lab_held))):
            move = pltpu.make_async_copy(
                store.at[episode, pl.ds(first, WIN + 16), :], held.at[k], sems.at[n, k]
            )
            move.start()
            moves.append(move)
    part = position_ref[1]
    for k in range(2):
        moves[2 * k].wait()
        moves[2 * k + 1].wait()
        wide[0, : WIN + 16] = lat_held[k].astype(F32)
        wide[1, : WIN + 16] = lab_held[k].astype(F32)
        for r in range(4):
            rows = wide[0, pl.ds(shifts[k] + r, PEERS, stride=4), :]
            pieces_ref[k, :, r * 128 : (r + 1) * 128] = rows.astype(BF)
        rows = wide[1, pl.ds(shifts[k] + part // 2, PEERS, stride=4), :]
        rows = jnp.where(part % 2 == 0, rows, pltpu.roll(rows, 64, 1))
        pieces_ref[k, :, 512:640] = rows.astype(BF)


def cut_windows(latents, labels, slot_source, episode_pick, window_start, position, part):
    smem = pl.BlockSpec(memory_space=pltpu.SMEM)
    vmem = pl.BlockSpec(memory_space=pltpu.VMEM)
    hbm = pl.BlockSpec(memory_space=pltpu.HBM)
    return pl.pallas_call(
        cut_kernel,
        out_shape=jax.ShapeDtypeStruct((2, PEERS, 640), BF),
        in_specs=[smem, vmem, vmem, vmem, hbm, hbm],
        out_specs=vmem,
        scratch_shapes=[
            pltpu.VMEM((2, WIN + 16, 128), BF),
            pltpu.VMEM((2, WIN + 16, 128), BF),
            pltpu.VMEM((2, WIN + 24, 128), F32),
            pltpu.SemaphoreType.DMA((2, 2)),
        ],
        compiler_params=pltpu.CompilerParams(vmem_limit_bytes=60 * 2**20),
        name="cut_windows",
    )(
        jnp.stack([position, part]),
        slot_source.reshape(1, 128),
        episode_pick.reshape(1, 128),
        window_start.reshape(1, 128),
        latents,
        labels,
    )


def order_kernel(arrived_ref, copies_ref, wide):
    for w in range(2):
        for r in range(4):
            wide[pl.ds(w * WIN + r, PEERS, stride=4), :] = arrived_ref[
                w, :, r * 128 : (r + 1) * 128
            ].astype(F32)
    first = arrived_ref[0, :, 512:640].astype(F32)
    second = pltpu.roll(arrived_ref[1, :, 512:640].astype(F32), 64, 1)
    lane = lax.broadcasted_iota(jnp.int32, (PEERS, 128), 1)
    both = jnp.where(lane < 64, first, second).astype(BF)
    rows = wide[...].astype(BF)
    for m in range(8):
        copies_ref[m, :512, :] = rows
        copies_ref[m, 512:576, :] = both
        copies_ref[m, 576:640, :] = jnp.zeros((64, 128), BF)


def order_rows(arrived):
    vmem = pl.BlockSpec(memory_space=pltpu.VMEM)
    return pl.pallas_call(
        order_kernel,
        out_shape=jax.ShapeDtypeStruct((8, 640, 128), BF),
        in_specs=[vmem],
        out_specs=vmem,
        scratch_shapes=[pltpu.VMEM((512, 128), F32)],
        compiler_params=pltpu.CompilerParams(vmem_limit_bytes=60 * 2**20),
        name="order_rows",
    )(arrived)


CHUNK = 128
ROWS = 512
SENT = 640


def two_parts(x):
    high = x.astype(BF).astype(F32)
    return high, x - high


def forward_kernel(
    place_ref, gathered_ref, own_ref, core_ref, gain_ref, head_ref,
    sent_ref, hidden_ref, inputs_ref, proj, scaled,
):
    xl, c = place_ref[0], place_ref[1]
    for zl in range(4):
        for zh in range(4):
            for dx in range(2):
                for dc, ref in enumerate((own_ref, core_ref)):
                    block = (zh * 4 + zl) * 4 + (xl ^ dx) * 2 + (c ^ dc)
                    proj[pl.ds(pl.multiple_of(block * 16, 16), 16), :] = ref[zl, dx, zh]
    for m in range(8):
        inputs_ref[:, m * 128 : (m + 1) * 128] = gathered_ref[m, :ROWS, :]
    gain = gain_ref[...]
    lane = lax.broadcasted_iota(jnp.int32, (CHUNK, 128), 1)
    row = lax.broadcasted_iota(jnp.int32, (16, 768), 0)
    gain_high, rest = two_parts(gain)
    gain_mid, gain_low = two_parts(rest)
    gains = jnp.where(
        row == 0, gain_high, jnp.where(row == 1, gain_mid, jnp.where(row == 2, gain_low, 0.0))
    )
    gain_head = jnp.sum(
        jnp.dot(gains.astype(BF), head_ref[...], preferred_element_type=F32), axis=0, keepdims=True
    )
    high, rest = two_parts(gain_head)
    mid, low = two_parts(rest)
    row = lax.broadcasted_iota(jnp.int32, (16, 128), 0)
    gain_head = jnp.where(row == 0, high, jnp.where(row == 1, mid, jnp.where(row == 2, low, 0.0)))
    for m in range(8):
        sent_ref[m, 576:592, :] = gain_head.astype(BF)
        sent_ref[m, 592:640, :] = jnp.zeros((48, 128), BF)

    for n in range(0, 768, 256):
        hidden_ref[:, n : n + 256] = jnp.dot(
            inputs_ref[...], proj[:, n : n + 256], preferred_element_type=F32
        )
    for i in range(0, ROWS, CHUNK):
        hidden = hidden_ref[i : i + CHUNK, :]
        mean = jnp.sum(hidden, axis=1, keepdims=True) / 768
        centred = hidden - mean
        square = jnp.sum(centred * centred, axis=1, keepdims=True)
        scaled[i : i + CHUNK, :] = (centred * gain).astype(BF)
        parts = []
        for value in (mean, square):
            high, rest = two_parts(value)
            mid, low = two_parts(rest)
            parts += [high, mid, low]
        packed = jnp.zeros((CHUNK, 128), F32)
        for k, value in enumerate(parts):
            packed = jnp.where(lane == k, value, packed)
        packed = packed.T[:16].astype(BF)
        start = ROWS + i // 8
        for m in range(8):
            sent_ref[m, start : start + 16, :] = packed
    partial = jnp.dot(scaled[...], head_ref[...], preferred_element_type=F32).astype(BF)
    for m in range(8):
        sent_ref[m, :ROWS, :] = partial


def backward_kernel(
    sent_ref, labels_ref, hidden_ref, gain_ref, head_ref,
    features_ref, back_ref, head_rows_ref, targets, errors, gain_sum,
):
    gain = gain_ref[...]
    lane = lax.broadcasted_iota(jnp.int32, (64, 128), 1)
    for r in range(4):
        one = labels_ref[2 * r].astype(F32)
        two = labels_ref[2 * r + 1].astype(F32)
        targets[pl.ds(r, 64, stride=4), :] = jnp.where(lane < 64, one, pltpu.roll(two, 64, 1))
        targets[pl.ds(WIN + r, 64, stride=4), :] = jnp.where(
            lane < 64, pltpu.roll(one, 64, 1), two
        )
    gain_heads = [
        jnp.sum(sent_ref[m, 576:592, :].astype(F32), axis=0, keepdims=True) for m in range(8)
    ]
    gain_head = sum(gain_heads)
    gain_sum[...] = jnp.zeros((8, 768), F32)
    lane = lax.broadcasted_iota(jnp.int32, (CHUNK, 128), 1) % 16

    for i in range(ROWS // CHUNK):
        rows = slice(i * CHUNK, (i + 1) * CHUNK)
        start = ROWS + i * 16
        stats = jnp.concatenate(
            [sent_ref[m, start : start + 16, :].astype(F32) for m in range(8)], axis=0
        ).T
        summed = sent_ref[0, rows, :].astype(F32)
        for m in range(1, 8):
            summed += sent_ref[m, rows, :].astype(F32)
        means = [
            jnp.sum(stats[:, 16 * m : 16 * m + 3], axis=1, keepdims=True) for m in range(8)
        ]
        mean = sum(means) / 8
        squares = jnp.sum(
            jnp.where((lane >= 3) & (lane < 6), stats, 0.0), axis=1, keepdims=True
        )
        for m in range(8):
            off = means[m] - mean
            squares += 768 * (off * off)
            summed += off * gain_heads[m]
        scale = lax.rsqrt(squares / D + EPSILON)
        predicted = scale * summed
        error = ((predicted - targets[rows, :]) / math.sqrt(32768)).astype(BF)
        errors[rows, :] = error
        wide = error.astype(F32)
        first = jnp.sum(wide * gain_head, axis=1, keepdims=True) / D
        second = jnp.sum(wide * predicted, axis=1, keepdims=True) / D
        normed = (hidden_ref[rows, :] - mean) * scale
        features_ref[rows, :] = (normed * gain).astype(BF)
        back = lax.dot_general(
            error, head_ref[...], (((1,), (1,)), ((), ())), preferred_element_type=F32
        )
        gain_sum[...] += jnp.sum((back * normed).reshape(CHUNK // 8, 8, 768), axis=0)
        back_ref[rows, :] = (scale * (back * gain - first - normed * second)).astype(BF)

    head_rows_ref[:, :768] = lax.dot_general(
        errors[...], features_ref[...], (((0,), (0,)), ((), ())), preferred_element_type=F32
    ).astype(BF)
    total = jnp.broadcast_to(jnp.sum(gain_sum[...], axis=0, keepdims=True), (8, 768))
    place = lax.broadcasted_iota(jnp.int32, (8, 128), 0)
    lane = lax.broadcasted_iota(jnp.int32, (8, 128), 1)
    for z in range(0, 16, 2):
        pair_rows = []
        for y in (z, z + 1):
            turned = total if y == 0 else pltpu.roll(total, 768 - 48 * y, 1)
            pair_rows.append(jnp.where((place == 0) & (lane < 48), turned[:, :128], 0.0))
        head_rows_ref[z * 8 : z * 8 + 16, 768:] = jnp.concatenate(pair_rows, axis=0).astype(BF)


def weight_kernel(place_ref, turned_ref, back_ref, kept_ref, given_ref, held):
    xl, c = place_ref[0], place_ref[1]
    for dc, out_ref in enumerate((kept_ref, given_ref)):
        for dx in range(2):
            for zl in range(4):
                for zh in range(4):
                    block = ((zh * 4 + zl) * 2 + (xl ^ dx)) * 2 + (c ^ dc)
                    row = dx * 256 + (zl * 4 + zh) * 16
                    held[dc, row : row + 16, :] = turned_ref[
                        pl.ds(pl.multiple_of(block * 16, 16), 16), :
                    ]
        for n in range(0, 768, 256):
            out_ref[:, n : n + 256] = jnp.dot(
                held[dc], back_ref[:, n : n + 256], preferred_element_type=F32
            ).astype(out_ref.dtype)


VMEM_SPEC = pl.BlockSpec(memory_space=pltpu.VMEM)
SMEM_SPEC = pl.BlockSpec(memory_space=pltpu.SMEM)


def call(kernel, name, outs, scratch, specs, *args):
    return pl.pallas_call(
        kernel,
        out_shape=outs,
        in_specs=specs,
        out_specs=jax.tree.map(lambda _: VMEM_SPEC, outs),
        scratch_shapes=scratch,
        compiler_params=pltpu.CompilerParams(vmem_limit_bytes=60 * 2**20),
        name=name,
    )(*args)


def array(shape, dtype):
    return jax.ShapeDtypeStruct(shape, dtype)


def on_device(
    latents, labels, slot_source, episode_pick, window_start, proj_weight, norm_gain, head_weight
):
    position = lax.axis_index("dp")
    c, xl, zl, zh = position % 2, (position // 2) % 2, (position // 4) % 4, position // 16
    pieces = cut_windows(
        latents, labels, slot_source, episode_pick, window_start, position, lax.axis_index("mp")
    )
    pieces = exchange(jnp.transpose(pieces, (1, 0, 2)), "dp")
    proj_own = gather(proj_weight, "dp", ZH_GROUPS)
    pieces, proj_own = tie(pieces, proj_own)
    proj_xlo = permute(proj_own, to_xlo)
    ordered = pieces.reshape(128, 640)[slot_source].reshape(PEERS, 2, 640)
    ordered, proj_own = tie(ordered, proj_own)
    arrived = exchange(ordered, "dp")
    proj_own = gather(jnp.concatenate([proj_own, proj_xlo]), "dp", ZL_GROUPS)
    proj_own = proj_own.reshape(4, 2, 4, 16, 768)
    arrived, proj_own = tie(arrived, proj_own)
    proj_core = permute(proj_own, to_core)
    gathered = exchange(order_rows(jnp.transpose(arrived, (1, 0, 2))), "mp")

    place = jnp.stack([xl, c])
    gain = norm_gain.reshape(1, 768)
    sent, hidden, inputs = call(
        forward_kernel,
        "forward",
        (array((8, SENT, 128), BF), array((ROWS, 768), F32), array((ROWS, 1024), BF)),
        [pltpu.VMEM((1024, 768), BF), pltpu.VMEM((ROWS, 768), BF)],
        [SMEM_SPEC] + [VMEM_SPEC] * 5,
        place, gathered, proj_own, proj_core, gain, head_weight,
    )
    all_sent = exchange(sent, "mp")
    features, back_hidden, head_rows = call(
        backward_kernel,
        "backward",
        (array((ROWS, 768), BF), array((ROWS, 768), BF), array((128, 896), BF)),
        [pltpu.VMEM((ROWS, 128), F32), pltpu.VMEM((ROWS, 128), BF), pltpu.VMEM((8, 768), F32)],
        [VMEM_SPEC] * 5,
        all_sent, gathered[:, 512:576], hidden, gain, head_weight,
    )
    kept, given = call(
        weight_kernel,
        "weight",
        (array((ROWS, 768), F32), array((ROWS, 768), BF)),
        [pltpu.VMEM((2, ROWS, ROWS), BF)],
        [SMEM_SPEC] + [VMEM_SPEC] * 2,
        place, jnp.transpose(inputs), back_hidden,
    )

    kept = kept + permute(given, to_core).astype(F32)
    head_rows, kept = tie(head_rows, kept)
    part = exchange(head_rows.reshape(16, 8, 896), "dp", Z_GROUPS)
    kept = kept[:256] + permute(kept[256:].astype(BF), to_xlo).astype(F32)
    kept = scatter4(kept.reshape(4, 64, 768), zl, to_zl)
    part, kept = tie(part, kept)
    part = jnp.sum(part.astype(F32), axis=0)
    part = part + permute(part, to_core)
    part = part + permute(part, to_xlo)
    grad_proj = exchange(kept.astype(BF).reshape(4, 16, 768), "dp", ZH_GROUPS)
    part, grad_proj = tie(part, grad_proj)
    grad_proj = jnp.sum(grad_proj.astype(F32), axis=0)
    whole = exchange(copies(part.astype(BF), 16), "dp", Z_GROUPS).astype(F32)
    grad_head = jnp.transpose(whole[:, :, :768].reshape(128, 768))
    grad_gain = whole[:, 0, 768:816].reshape(768)
    return (grad_proj, grad_head, grad_gain, features)


def solution(mesh):
    in_specs = (
        P("dp", None, "mp"),
        P("dp", None, None),
        P(),
        P(),
        P(),
        P("dp", "mp"),
        P("mp"),
        P("mp", None),
    )
    out_specs = (P("dp", "mp"), P("mp", None), P("mp"), P("dp", "mp"))
    return jax.shard_map(
        on_device, mesh=mesh, in_specs=in_specs, out_specs=out_specs, check_vma=False
    )
```

time: 267 us -> 241 us (0.903)
  the two profiles are of different devices: /device:TPU:4 before, /device:TPU:34 now
where the time goes in v2:
time: 241 us; the launch traced here: 240 us
  starting transfers between devices  92.9 us (39%)
  waiting for transfers between devices  67.9 us (28%)
  blocking collectives  41.3 us (17%)
  Pallas kernels  20.6 us (9%)
  local copies, waits for them, and re-layouts  12.3 us (5%)
  other arithmetic  4.27 us (2%)
    all_to_all x7, starting transfers between devices, exchange(): lax.all_to_all(x, axis, split_axis=0, concat_axis=0, tiled=True, axis_ind...  68.5 us
    all_to_all x7, waiting for transfers between devices, exchange(): lax.all_to_all(x, axis, split_axis=0, concat_axis=0, tiled=True, axis_ind...  48.6 us
    all_gather x2, blocking collectives, gather(): return lax.all_gather(x, axis, axis=0, tiled=True, axis_index_groups=groups)  41.3 us
    ppermute x9, starting transfers between devices, permute(): return lax.ppermute(x, 'dp', [(i, target(i)) for i in range(N_DP)])  24.4 us
    ppermute x9, waiting for transfers between devices, permute(): return lax.ppermute(x, 'dp', [(i, target(i)) for i in range(N_DP)])  19.3 us
    pallas_call x3, Pallas kernels, call(): pl.pallas_call(kernel, out_shape=outs, in_specs=specs, out_specs=jax.tree...  15.7 us
  transfers between devices with their start and end apart: 16, of which 11 were waited for; matrix products, arithmetic and copies ran while one was open for 2% of the time, Pallas kernels for 0%

profile of v2, /device:TPU:34, one launch (start us, length us, event | category | flops | bytes accessed | tf_op | source)
XLA Modules:
  0.0 240.1 jit_solution(14506409236315295836)
XLA Ops:
  1.2 2.8 %cut_windows.1 = bf16[2,64,640]{2,1,0:T(8,128)(2,1)} custom-call(s32[2]{0:T(128)} %pad_add_fusion.1.position_ref, s32[1,128]{1,0:T(1,128)} %bitcast.41, s32[1,128]{1,0:T(1,128)} %bitcast.39, s32[1,128]{1,0:T(1,128)} %bitcast.40, bf16[8,512,128]{2,1,0:T(8,128)(2,1)} %latents_ref.1, bf16[8,512,128]{2,1,0:T(8,128)(2,1)} %labels_ref.1), custom_call_target="tpu_custom_call" | custom-call | tf_op jit(solution)/shard_map/cut_windows/pallas_call | solution.py:114
  4.0 1.8 copy.17
  5.8 16.7 %all-to-all-start = ((bf16[64,2,640]{2,1,0:T(2,128)(2,1)}), bf16[64,2,640]{2,1,0:T(2,128)(2,1)S(1)}, u32[]{:S(2)}, u32[]{:S(2)}) async-start(bf16[64,2,640]{2,1,0:T(2,128)(2,1)} %copy.17), calls=%async_computation | async-start | bytes 327680 | tf_op jit(solution)/shard_map/all_to_all | solution.py:43
  22.4 23.2 %all_gather.6 = bf16[64,768]{1,0:T(8,128)(2,1)S(1)} all-gather(bf16[16,768]{1,0:T(8,128)(2,1)S(1)} %copy-done.5), channel_id=1, replica_groups={{0,128,256,384},{8,136,264,392},{16,144,272,400},{24,152,280,408},{32,1..., dimensions={0}, use_global_device_ids=true | all-gather | bytes 122880 | tf_op jit(solution)/shard_map/all_gather | solution.py:49
  45.7 0.9 gather_fusion
  46.6 0.7 reshape.49
  47.4 9.1 %all-to-all-start.1 = ((bf16[64,2,640]{2,1,0:T(2,128)(2,1)}), bf16[64,2,640]{2,1,0:T(2,128)(2,1)S(1)}, u32[]{:S(2)}, u32[]{:S(2)}) async-start(bf16[64,2,640]{2,1,0:T(2,128)(2,1)} %reshape.49), calls=%async_computation.1 | async-start | bytes 327680 | tf_op jit(solution)/shard_map/all_to_all | solution.py:43
  56.5 2.5 %collective-permute-start = (bf16[64,768]{1,0:T(8,128)(2,1)S(1)}, bf16[64,768]{1,0:T(8,128)(2,1)S(1)}, u32[]{:S(2)}, u32[]{:S(2)}) collective-permute-start(bf16[64,768]{1,0:T(8,128)(2,1)S(1)} %all_gather.6), channel_id=1, source_target_pairs={{0,16},{8,24},{16,0},{24,8},{32,48},{40,56},{48,32},{56,40},{64,80... | collective-permute-start | bytes 294920 | tf_op jit(solution)/shard_map/ppermute | solution.py:39
  59.0 4.6 %collective-permute-done = bf16[64,768]{1,0:T(8,128)(2,1)S(1)} collective-permute-done((bf16[64,768]{1,0:T(8,128)(2,1)S(1)}, bf16[64,768]{1,0:T(8,128)(2,1)S(1)}, u32[]{:S(2)}, u32[]{:S(2)}) %collective-permute-start) | collective-permute-done | bytes 98336 | tf_op jit(solution)/shard_map/ppermute | solution.py:39
  63.6 18.1 %all_gather.7 = bf16[512,768]{1,0:T(8,128)(2,1)S(1)} all-gather(bf16[128,768]{1,0:T(8,128)(2,1)S(1)} %pad_maximum_fusion), channel_id=1, replica_groups={{0,32,64,96},{8,40,72,104},{16,48,80,112},{24,56,88,120},{128,160,192,2..., dimensions={0}, use_global_device_ids=true | all-gather | bytes 983040 | tf_op jit(solution)/shard_map/all_gather | solution.py:49
  81.7 0.7 copy.22
  82.4 2.1 order_rows.1
  84.5 6.2 %all-to-all-start.2 = ((bf16[8,640,128]{2,1,0:T(8,128)(2,1)}), bf16[8,640,128]{2,1,0:T(8,128)(2,1)S(1)}, u32[]{:S(2)}, u32[]{:S(2)}) async-start(bf16[8,640,128]{2,1,0:T(8,128)(2,1)} %order_rows.1), calls=%async_computation.2 | async-start | bytes 2621440 | tf_op jit(solution)/shard_map/all_to_all | solution.py:43
  90.7 1.9 collective-permute-start.1
  93.3 0.6 pad_add_fusion.place_ref
  93.9 1.0 collective-permute-done.1.core_ref
  94.9 13.4 %all-to-all-done.2.gathered_ref = bf16[8,640,128]{2,1,0:T(8,128)(2,1)S(1)} async-done(((bf16[8,640,128]{2,1,0:T(8,128)(2,1)}), bf16[8,640,128]{2,1,0:T(8,128)(2,1)S(1)}, u32[]{:S(2)}, u32[]{:S(2)}) %all-to-all-start.2) | async-done | bytes 1310752 | tf_op jit(solution)/shard_map/all_to_all | solution.py:43
  108.2 1.1 copy-done
  109.3 5.2 %forward.1 = (bf16[8,640,128]{2,1,0:T(8,128)(2,1)}, f32[512,768]{1,0:T(8,128)}, bf16[512,1024]{1,0:T(8,128)(2,1)}) custom-call(s32[2]{0:T(128)} %pad_add_fusion.place_ref, bf16[8,640,128]{2,1,0:T(8,128)(2,1)} %copy-done, bf16[4,2,4,16,768]{4,3,2,1,0:T(8,128)(2,1)} %bitcast.34, bf16[4,2,4,16,768]{4,3,2,1,0:T(8,128)(2,1)} %copy-done.4, ...), custom_call_target="tpu_custom_call" | custom-call | tf_op jit(solution)/shard_map/forward/pallas_call | solution.py:327
  114.5 3.7 %all-to-all-start.3 = ((bf16[8,640,128]{2,1,0:T(8,128)(2,1)}), bf16[8,640,128]{2,1,0:T(8,128)(2,1)S(1)}, u32[]{:S(2)}, u32[]{:S(2)}) async-start(bf16[8,640,128]{2,1,0:T(8,128)(2,1)} %get-tuple-element.30), calls=%async_computation.3 | async-start | bytes 2621440 | tf_op jit(solution)/shard_map/all_to_all | solution.py:43
  118.2 1.3 copy.19
  119.5 1.6 slice.23.labels_ref
  121.1 14.4 %all-to-all-done.3.sent_ref = bf16[8,640,128]{2,1,0:T(8,128)(2,1)S(1)} async-done(((bf16[8,640,128]{2,1,0:T(8,128)(2,1)}), bf16[8,640,128]{2,1,0:T(8,128)(2,1)S(1)}, u32[]{:S(2)}, u32[]{:S(2)}) %all-to-all-start.3) | async-done | bytes 1310752 | tf_op jit(solution)/shard_map/all_to_all | solution.py:43
  135.5 1.1 copy-done.1
  136.6 6.9 %backward.1 = (bf16[512,768]{1,0:T(8,128)(2,1)}, bf16[512,768]{1,0:T(8,128)(2,1)}, bf16[128,896]{1,0:T(8,128)(2,1)}) custom-call(bf16[8,640,128]{2,1,0:T(8,128)(2,1)} %copy-done.1, bf16[8,64,128]{2,1,0:T(8,128)(2,1)} %slice.23.labels_ref, f32[512,768]{1,0:T(8,128)} %get-tuple-element.31.hidden_ref, f32[1,768]{1,0:T(1,128)} %reshape.51.gain_ref, ...), custom_call_target="tpu_custom_call" | custom-call | tf_op jit(solution)/shard_map/backward/pallas_call | solution.py:327
  143.5 3.6 %weight.1 = (f32[512,768]{1,0:T(8,128)}, bf16[512,768]{1,0:T(8,128)(2,1)}) custom-call(s32[2]{0:T(128)} %pad_add_fusion.place_ref, bf16[1024,512]{1,0:T(8,128)(2,1)} %bitcast.32, bf16[512,768]{1,0:T(8,128)(2,1)} %get-tuple-element.34.back_ref), custom_call_target="tpu_custom_call" | custom-call | tf_op jit(solution)/shard_map/weight/pallas_call | solution.py:327
  147.1 1.9 collective-permute-start.2
  149.1 2.5 %collective-permute-done.2 = bf16[512,768]{1,0:T(8,128)(2,1)S(1)} collective-permute-done((bf16[512,768]{1,0:T(8,128)(2,1)}, bf16[512,768]{1,0:T(8,128)(2,1)S(1)}, u32[]{:S(2)}, u32[]{:S(2)}) %collective-permute-start.2) | collective-permute-done | bytes 786464 | tf_op jit(solution)/shard_map/ppermute | solution.py:39
  151.5 1.6 convert_add_fusion
  153.2 2.7 %collective-permute-start.3 = (bf16[256,768]{1,0:T(8,128)(2,1)S(1)}, bf16[256,768]{1,0:T(8,128)(2,1)S(1)}, u32[]{:S(2)}, u32[]{:S(2)}) collective-permute-start(bf16[256,768]{1,0:T(8,128)(2,1)S(1)} %slice.31), channel_id=1, source_target_pairs={{0,16},{8,24},{16,0},{24,8},{32,48},{40,56},{48,32},{56,40},{64,80... | collective-permute-start | bytes 1179656 | tf_op jit(solution)/shard_map/ppermute | solution.py:39
  155.9 12.1 %all-to-all-start.4 = ((bf16[16,8,896]{2,1,0:T(8,128)(2,1)}), bf16[16,8,896]{2,1,0:T(8,128)(2,1)S(1)}, u32[]{:S(2)}, u32[]{:S(2)}) async-start(bf16[16,8,896]{2,1,0:T(8,128)(2,1)} %bitcast.11), calls=%async_computation.4 | async-start | bytes 458752 | tf_op jit(solution)/shard_map/all_to_all | solution.py:43
  168.1 2.1 collective-permute-start.6
  170.2 4.6 %collective-permute-start.5 = (bf16[64,768]{1,0:T(8,128)(2,1)S(1)}, bf16[64,768]{1,0:T(8,128)(2,1)S(1)}, u32[]{:S(2)}, u32[]{:S(2)}) collective-permute-start(bf16[64,768]{1,0:T(8,128)(2,1)S(1)} %get-tuple-element.54), channel_id=1, source_target_pairs={{0,64},{8,72},{16,80},{24,88},{32,96},{40,104},{48,112},{56,120},{... | collective-permute-start | bytes 294920 | tf_op jit(solution)/shard_map/ppermute | solution.py:39
  174.9 4.3 %collective-permute-start.4 = (bf16[64,768]{1,0:T(8,128)(2,1)S(1)}, bf16[64,768]{1,0:T(8,128)(2,1)S(1)}, u32[]{:S(2)}, u32[]{:S(2)}) collective-permute-start(bf16[64,768]{1,0:T(8,128)(2,1)S(1)} %get-tuple-element.52), channel_id=1, source_target_pairs={{0,32},{8,40},{16,48},{24,56},{32,64},{40,72},{48,80},{56,88},{64,... | collective-permute-start | bytes 294920 | tf_op jit(solution)/shard_map/ppermute | solution.py:39
  179.1 6.6 %collective-permute-done.6 = bf16[64,768]{1,0:T(8,128)(2,1)S(1)} collective-permute-done((bf16[64,768]{1,0:T(8,128)(2,1)S(1)}, bf16[64,768]{1,0:T(8,128)(2,1)S(1)}, u32[]{:S(2)}, u32[]{:S(2)}) %collective-permute-start.6) | collective-permute-done | bytes 98336 | tf_op jit(solution)/shard_map/ppermute | solution.py:39
  185.8 0.7 fusion.1
  186.5 10.8 %all-to-all-start.5 = ((bf16[4,16,768]{2,1,0:T(8,128)(2,1)}), bf16[4,16,768]{2,1,0:T(8,128)(2,1)S(1)}, u32[]{:S(2)}, u32[]{:S(2)}) async-start(bf16[4,16,768]{2,1,0:T(8,128)(2,1)} %bitcast.17), calls=%async_computation.5 | async-start | bytes 196608 | tf_op jit(solution)/shard_map/all_to_all | solution.py:43
  197.4 1.9 collective-permute-start.7
  199.3 1.2 collective-permute-done.7
  200.5 2.4 %collective-permute-start.8 = (f32[8,896]{1,0:T(8,128)S(1)}, f32[8,896]{1,0:T(8,128)S(1)}, u32[]{:S(2)}, u32[]{:S(2)}) collective-permute-start(f32[8,896]{1,0:T(8,128)S(1)} %add.90), channel_id=1, source_target_pairs={{0,16},{8,24},{16,0},{24,8},{32,48},{40,56},{48,32},{56,40},{64,80... | collective-permute-start | bytes 86024 | tf_op jit(solution)/shard_map/ppermute | solution.py:39
  202.9 3.3 %collective-permute-done.8 = f32[8,896]{1,0:T(8,128)S(1)} collective-permute-done((f32[8,896]{1,0:T(8,128)S(1)}, f32[8,896]{1,0:T(8,128)S(1)}, u32[]{:S(2)}, u32[]{:S(2)}) %collective-permute-start.8) | collective-permute-done | bytes 28704 | tf_op jit(solution)/shard_map/ppermute | solution.py:39
  206.2 4.5 %all-to-all-done.5 = bf16[4,16,768]{2,1,0:T(8,128)(2,1)S(1)} async-done(((bf16[4,16,768]{2,1,0:T(8,128)(2,1)}), bf16[4,16,768]{2,1,0:T(8,128)(2,1)S(1)}, u32[]{:S(2)}, u32[]{:S(2)}) %all-to-all-start.5) | async-done | bytes 98336 | tf_op jit(solution)/shard_map/all_to_all | solution.py:43
  210.8 0.7 broadcast_in_dim.10
  211.5 10.0 %all-to-all-start.6 = ((bf16[16,8,896]{2,1,0:T(8,128)(2,1)}), bf16[16,8,896]{2,1,0:T(8,128)(2,1)S(1)}, u32[]{:S(2)}, u32[]{:S(2)}) async-start(bf16[16,8,896]{2,1,0:T(8,128)(2,1)} %broadcast_in_dim.10), calls=%async_computation.6 | async-start | bytes 458752 | tf_op jit(solution)/shard_map/all_to_all | solution.py:43
  221.5 0.6 convert_reduce_fusion.1
  222.1 16.3 %all-to-all-done.6 = bf16[16,8,896]{2,1,0:T(8,128)(2,1)S(1)} async-done(((bf16[16,8,896]{2,1,0:T(8,128)(2,1)}), bf16[16,8,896]{2,1,0:T(8,128)(2,1)S(1)}, u32[]{:S(2)}, u32[]{:S(2)}) %all-to-all-start.6) | async-done | bytes 229408 | tf_op jit(solution)/shard_map/all_to_all | solution.py:43
  238.5 0.9 copy.20
  239.4 0.7 reshape_squeeze.3
  (35 shorter events, 1.7 us)
Async XLA Ops:
  0.6 45.0 %copy-start.7 = (s32[128]{0:T(128)S(1)}, s32[128]{0:T(128)}, u32[]{:S(2)}) copy-start(s32[128]{0:T(128)} %param.10) | copy-start | bytes 1540
  0.6 21.8 %copy-start.5 = (bf16[16,768]{1,0:T(8,128)(2,1)S(1)}, bf16[16,768]{1,0:T(8,128)(2,1)}, u32[]{:S(2)}) copy-start(bf16[16,768]{1,0:T(8,128)(2,1)} %param.13) | copy-start | bytes 73732
  5.8 39.9 %all-to-all-start = ((bf16[64,2,640]{2,1,0:T(2,128)(2,1)}), bf16[64,2,640]{2,1,0:T(2,128)(2,1)S(1)}, u32[]{:S(2)}, u32[]{:S(2)}) async-start(bf16[64,2,640]{2,1,0:T(2,128)(2,1)} %copy.17), calls=%async_computation | async-start | bytes 327680 | tf_op jit(solution)/shard_map/all_to_all | solution.py:43
  47.4 34.3 %all-to-all-start.1 = ((bf16[64,2,640]{2,1,0:T(2,128)(2,1)}), bf16[64,2,640]{2,1,0:T(2,128)(2,1)S(1)}, u32[]{:S(2)}, u32[]{:S(2)}) async-start(bf16[64,2,640]{2,1,0:T(2,128)(2,1)} %reshape.49), calls=%async_computation.1 | async-start | bytes 327680 | tf_op jit(solution)/shard_map/all_to_all | solution.py:43
  56.5 7.1 %collective-permute-start = (bf16[64,768]{1,0:T(8,128)(2,1)S(1)}, bf16[64,768]{1,0:T(8,128)(2,1)S(1)}, u32[]{:S(2)}, u32[]{:S(2)}) collective-permute-start(bf16[64,768]{1,0:T(8,128)(2,1)S(1)} %all_gather.6), channel_id=1, source_target_pairs={{0,16},{8,24},{16,0},{24,8},{32,48},{40,56},{48,32},{56,40},{64,80... | collective-permute-start | bytes 294920 | tf_op jit(solution)/shard_map/ppermute | solution.py:39
  81.7 9.0 %copy-start.2 = (bf16[512,768]{1,0:T(8,128)(2,1)}, bf16[512,768]{1,0:T(8,128)(2,1)S(1)}, u32[]{:S(2)}) copy-start(bf16[512,768]{1,0:T(8,128)(2,1)S(1)} %all_gather.7) | copy-start | bytes 2359300
  84.5 8.1 %copy-start.6 = (f32[768]{0:T(1024)S(1)}, f32[768]{0:T(1024)}, u32[]{:S(2)}) copy-start(f32[768]{0:T(1024)} %param.14) | copy-start | bytes 9220
  84.5 23.7 %all-to-all-start.2 = ((bf16[8,640,128]{2,1,0:T(8,128)(2,1)}), bf16[8,640,128]{2,1,0:T(8,128)(2,1)S(1)}, u32[]{:S(2)}, u32[]{:S(2)}) async-start(bf16[8,640,128]{2,1,0:T(8,128)(2,1)} %order_rows.1), calls=%async_computation.2 | async-start | bytes 2621440 | tf_op jit(solution)/shard_map/all_to_all | solution.py:43
  90.7 4.2 %collective-permute-start.1 = (bf16[4,2,4,16,768]{4,3,2,1,0:T(8,128)(2,1)S(1)}, bf16[4,2,4,16,768]{4,3,2,1,0:T(8,128)(2,1)S(1)}, u32[]{:S(2)}, u32[]{:S(2)}) collective-permute-start(bf16[4,2,4,16,768]{4,3,2,1,0:T(8,128)(2,1)S(1)} %bitcast.33), channel_id=1, source_target_pairs={{0,8},{8,0},{16,24},{24,16},{32,40},{40,32},{48,56},{56,48},{64,72... | collective-permute-start | bytes 2359304 | tf_op jit(solution)/shard_map/ppermute | solution.py:39
  94.9 13.4 %copy-start.4 = (bf16[4,2,4,16,768]{4,3,2,1,0:T(8,128)(2,1)}, bf16[4,2,4,16,768]{4,3,2,1,0:T(8,128)(2,1)S(1)}, u32[]{:S(2)}) copy-start(bf16[4,2,4,16,768]{4,3,2,1,0:T(8,128)(2,1)S(1)} %collective-permute-done.1.core_ref) | copy-start | bytes 2359300
  108.2 1.1 copy-start
  114.5 3.7 %copy-start.3 = (bf16[512,1024]{1,0:T(8,128)(2,1)S(1)}, bf16[512,1024]{1,0:T(8,128)(2,1)}, u32[]{:S(2)}) copy-start(bf16[512,1024]{1,0:T(8,128)(2,1)} %get-tuple-element.33) | copy-start | bytes 3145732
  114.5 21.0 %all-to-all-start.3 = ((bf16[8,640,128]{2,1,0:T(8,128)(2,1)}), bf16[8,640,128]{2,1,0:T(8,128)(2,1)S(1)}, u32[]{:S(2)}, u32[]{:S(2)}) async-start(bf16[8,640,128]{2,1,0:T(8,128)(2,1)} %get-tuple-element.30), calls=%async_computation.3 | async-start | bytes 2621440 | tf_op jit(solution)/shard_map/all_to_all | solution.py:43
  135.5 1.1 copy-start.1
  147.1 4.4 %collective-permute-start.2 = (bf16[512,768]{1,0:T(8,128)(2,1)}, bf16[512,768]{1,0:T(8,128)(2,1)S(1)}, u32[]{:S(2)}, u32[]{:S(2)}) collective-permute-start(bf16[512,768]{1,0:T(8,128)(2,1)} %get-tuple-element.36), channel_id=1, source_target_pairs={{0,8},{8,0},{16,24},{24,16},{32,40},{40,32},{48,56},{56,48},{64,72... | collective-permute-start | bytes 2359304 | tf_op jit(solution)/shard_map/ppermute | solution.py:39
  153.2 14.8 %collective-permute-start.3 = (bf16[256,768]{1,0:T(8,128)(2,1)S(1)}, bf16[256,768]{1,0:T(8,128)(2,1)S(1)}, u32[]{:S(2)}, u32[]{:S(2)}) collective-permute-start(bf16[256,768]{1,0:T(8,128)(2,1)S(1)} %slice.31), channel_id=1, source_target_pairs={{0,16},{8,24},{16,0},{24,8},{32,48},{40,56},{48,32},{56,40},{64,80... | collective-permute-start | bytes 1179656 | tf_op jit(solution)/shard_map/ppermute | solution.py:39
  155.9 30.6 %all-to-all-start.4 = ((bf16[16,8,896]{2,1,0:T(8,128)(2,1)}), bf16[16,8,896]{2,1,0:T(8,128)(2,1)S(1)}, u32[]{:S(2)}, u32[]{:S(2)}) async-start(bf16[16,8,896]{2,1,0:T(8,128)(2,1)} %bitcast.11), calls=%async_computation.4 | async-start | bytes 458752 | tf_op jit(solution)/shard_map/all_to_all | solution.py:43
  168.1 17.7 %collective-permute-start.6 = (bf16[64,768]{1,0:T(8,128)(2,1)S(1)}, bf16[64,768]{1,0:T(8,128)(2,1)S(1)}, u32[]{:S(2)}, u32[]{:S(2)}) collective-permute-start(bf16[64,768]{1,0:T(8,128)(2,1)S(1)} %get-tuple-element.53), channel_id=1, source_target_pairs={{0,96},{8,104},{16,112},{24,120},{32,0},{40,8},{48,16},{56,24},{64... | collective-permute-start | bytes 294920 | tf_op jit(solution)/shard_map/ppermute | solution.py:39
  170.2 15.6 %collective-permute-start.5 = (bf16[64,768]{1,0:T(8,128)(2,1)S(1)}, bf16[64,768]{1,0:T(8,128)(2,1)S(1)}, u32[]{:S(2)}, u32[]{:S(2)}) collective-permute-start(bf16[64,768]{1,0:T(8,128)(2,1)S(1)} %get-tuple-element.54), channel_id=1, source_target_pairs={{0,64},{8,72},{16,80},{24,88},{32,96},{40,104},{48,112},{56,120},{... | collective-permute-start | bytes 294920 | tf_op jit(solution)/shard_map/ppermute | solution.py:39
  174.9 11.0 %collective-permute-start.4 = (bf16[64,768]{1,0:T(8,128)(2,1)S(1)}, bf16[64,768]{1,0:T(8,128)(2,1)S(1)}, u32[]{:S(2)}, u32[]{:S(2)}) collective-permute-start(bf16[64,768]{1,0:T(8,128)(2,1)S(1)} %get-tuple-element.52), channel_id=1, source_target_pairs={{0,32},{8,40},{16,48},{24,56},{32,64},{40,72},{48,80},{56,88},{64,... | collective-permute-start | bytes 294920 | tf_op jit(solution)/shard_map/ppermute | solution.py:39
  186.5 24.3 %all-to-all-start.5 = ((bf16[4,16,768]{2,1,0:T(8,128)(2,1)}), bf16[4,16,768]{2,1,0:T(8,128)(2,1)S(1)}, u32[]{:S(2)}, u32[]{:S(2)}) async-start(bf16[4,16,768]{2,1,0:T(8,128)(2,1)} %bitcast.17), calls=%async_computation.5 | async-start | bytes 196608 | tf_op jit(solution)/shard_map/all_to_all | solution.py:43
  197.4 3.1 %collective-permute-start.7 = (f32[8,896]{1,0:T(8,128)S(1)}, f32[8,896]{1,0:T(8,128)S(1)}, u32[]{:S(2)}, u32[]{:S(2)}) collective-permute-start(f32[8,896]{1,0:T(8,128)S(1)} %convert_reduce_fusion), channel_id=1, source_target_pairs={{0,8},{8,0},{16,24},{24,16},{32,40},{40,32},{48,56},{56,48},{64,72... | collective-permute-start | bytes 86024 | tf_op jit(solution)/shard_map/ppermute | solution.py:39
  200.5 5.8 %collective-permute-start.8 = (f32[8,896]{1,0:T(8,128)S(1)}, f32[8,896]{1,0:T(8,128)S(1)}, u32[]{:S(2)}, u32[]{:S(2)}) collective-permute-start(f32[8,896]{1,0:T(8,128)S(1)} %add.90), channel_id=1, source_target_pairs={{0,16},{8,24},{16,0},{24,8},{32,48},{40,56},{48,32},{56,40},{64,80... | collective-permute-start | bytes 86024 | tf_op jit(solution)/shard_map/ppermute | solution.py:39
  211.5 26.9 %all-to-all-start.6 = ((bf16[16,8,896]{2,1,0:T(8,128)(2,1)}), bf16[16,8,896]{2,1,0:T(8,128)(2,1)S(1)}, u32[]{:S(2)}, u32[]{:S(2)}) async-start(bf16[16,8,896]{2,1,0:T(8,128)(2,1)} %broadcast_in_dim.10), calls=%async_computation.6 | async-start | bytes 458752 | tf_op jit(solution)/shard_map/all_to_all | solution.py:43

commit v3 on v2

--- a/solution.py
+++ b/solution.py
@@ -59,14 +59,6 @@
 
 def pair(mine, other, index):
     return jnp.where(index == 0, jnp.stack([mine, other]), jnp.stack([other, mine]))
-
-
-def scatter4(blocks, index, to):
-    total = take(blocks, index, 0)
-    for k in (1, 2, 3):
-        sent = take(blocks, (index + k) % 4, 0).astype(BF)
-        total = total + permute(sent, to(k)).astype(F32)
-    return total
 
 
 def tie(x, y):
@@ -251,29 +243,24 @@
     ]
     gain_head = sum(gain_heads)
     gain_sum[...] = jnp.zeros((8, 768), F32)
-    lane = lax.broadcasted_iota(jnp.int32, (CHUNK, 128), 1) % 16
 
     for i in range(ROWS // CHUNK):
         rows = slice(i * CHUNK, (i + 1) * CHUNK)
         start = ROWS + i * 16
-        stats = jnp.concatenate(
-            [sent_ref[m, start : start + 16, :].astype(F32) for m in range(8)], axis=0
-        ).T
+        stats = [sent_ref[m, start : start + 16, :].astype(F32) for m in range(8)]
+        means = [part[0:1] + part[1:2] + part[2:3] for part in stats]
+        mean = sum(means) / 8
+        offs = [value - mean for value in means]
+        squares = sum(part[3:4] + part[4:5] + part[5:6] for part in stats)
+        squares += 768 * sum(off * off for off in offs)
+        scale = lax.rsqrt(squares / D + EPSILON)
+        turned = jnp.concatenate(offs + [mean, scale, jnp.zeros((118, 128), F32)], axis=0).T
+        mean, scale = turned[:, 8:9], turned[:, 9:10]
         summed = sent_ref[0, rows, :].astype(F32)
         for m in range(1, 8):
             summed += sent_ref[m, rows, :].astype(F32)
-        means = [
-            jnp.sum(stats[:, 16 * m : 16 * m + 3], axis=1, keepdims=True) for m in range(8)
-        ]
-        mean = sum(means) / 8
-        squares = jnp.sum(
-            jnp.where((lane >= 3) & (lane < 6), stats, 0.0), axis=1, keepdims=True
-        )
         for m in range(8):
-            off = means[m] - mean
-            squares += 768 * (off * off)
-            summed += off * gain_heads[m]
-        scale = lax.rsqrt(squares / D + EPSILON)
+            summed += turned[:, m : m + 1] * gain_heads[m]
         predicted = scale * summed
         error = ((predicted - targets[rows, :]) / math.sqrt(32768)).astype(BF)
         errors[rows, :] = error
@@ -392,15 +379,18 @@
     head_rows, kept = tie(head_rows, kept)
     part = exchange(head_rows.reshape(16, 8, 896), "dp", Z_GROUPS)
     kept = kept[:256] + permute(kept[256:].astype(BF), to_xlo).astype(F32)
-    kept = scatter4(kept.reshape(4, 64, 768), zl, to_zl)
-    part, kept = tie(part, kept)
+    blocks = kept.reshape(4, 64, 768)
+    from_zl = [permute(take(blocks, (zl + k) % 4, 0).astype(BF), to_zl(k)) for k in (1, 2, 3)]
+    part, first = tie(part, from_zl[0])
     part = jnp.sum(part.astype(F32), axis=0)
     part = part + permute(part, to_core)
+    kept = take(blocks, zl, 0)
+    for block in (first, from_zl[1], from_zl[2]):
+        kept = kept + block.astype(F32)
     part = part + permute(part, to_xlo)
     grad_proj = exchange(kept.astype(BF).reshape(4, 16, 768), "dp", ZH_GROUPS)
-    part, grad_proj = tie(part, grad_proj)
     grad_proj = jnp.sum(grad_proj.astype(F32), axis=0)
-    whole = exchange(copies(part.astype(BF), 16), "dp", Z_GROUPS).astype(F32)
+    whole = gather(part, "dp", Z_GROUPS).reshape(16, 8, 896)
     grad_head = jnp.transpose(whole[:, :, :768].reshape(128, 768))
     grad_gain = whole[:, 0, 768:816].reshape(768)
     return (grad_proj, grad_head, grad_gain, features)

time: 241 us -> 238 us (0.988)
  the two profiles are of different devices: /device:TPU:34 before, /device:TPU:32 now
where the time goes in v3:
time: 238 us; the launch traced here: 237 us
  starting transfers between devices  80.6 us (34%)
  blocking collectives  78.2 us (33%)
  waiting for transfers between devices  43.1 us (18%)
  Pallas kernels  18.8 us (8%)
  local copies, waits for them, and re-layouts  11.5 us (5%)
  other arithmetic  4.26 us (2%)
    all_gather x3, blocking collectives, gather(): return lax.all_gather(x, axis, axis=0, tiled=True, axis_index_groups=groups)  78.2 us
    all_to_all x6, starting transfers between devices, exchange(): lax.all_to_all(x, axis, split_axis=0, concat_axis=0, tiled=True, axis_ind...  54.9 us
    all_to_all x6, waiting for transfers between devices, exchange(): lax.all_to_all(x, axis, split_axis=0, concat_axis=0, tiled=True, axis_ind...  33 us
    ppermute x9, starting transfers between devices, permute(): return lax.ppermute(x, 'dp', [(i, target(i)) for i in range(N_DP)])  25.8 us
    pallas_call x3, Pallas kernels, call(): pl.pallas_call(kernel, out_shape=outs, in_specs=specs, out_specs=jax.tree...  13.9 us
    ppermute x9, waiting for transfers between devices, permute(): return lax.ppermute(x, 'dp', [(i, target(i)) for i in range(N_DP)])  10.1 us
  transfers between devices with their start and end apart: 15, of which 8 were waited for; matrix products, arithmetic and copies ran while one was open for 3% of the time, Pallas kernels for 0%

profile of v3, /device:TPU:32, one launch (start us, length us, event | category | flops | bytes accessed | tf_op | source)
XLA Modules:
  0.0 237.4 jit_solution(13487831165922222927)
XLA Ops:
  0.7 0.6 pad_add_fusion.1.position_ref
  1.2 2.8 %cut_windows.1 = bf16[2,64,640]{2,1,0:T(8,128)(2,1)} custom-call(s32[2]{0:T(128)} %pad_add_fusion.1.position_ref, s32[1,128]{1,0:T(1,128)} %bitcast.46, s32[1,128]{1,0:T(1,128)} %bitcast.44, s32[1,128]{1,0:T(1,128)} %bitcast.45, bf16[8,512,128]{2,1,0:T(8,128)(2,1)} %latents_ref.1, bf16[8,512,128]{2,1,0:T(8,128)(2,1)} %labels_ref.1), custom_call_target="tpu_custom_call" | custom-call | tf_op jit(solution)/shard_map/cut_windows/pallas_call | solution.py:106
  4.0 1.8 copy.17
  5.8 16.7 %all-to-all-start = ((bf16[64,2,640]{2,1,0:T(2,128)(2,1)}), bf16[64,2,640]{2,1,0:T(2,128)(2,1)S(1)}, u32[]{:S(2)}, u32[]{:S(2)}) async-start(bf16[64,2,640]{2,1,0:T(2,128)(2,1)} %copy.17), calls=%async_computation | async-start | bytes 327680 | tf_op jit(solution)/shard_map/all_to_all | solution.py:43
  22.5 23.3 %all_gather.9 = bf16[64,768]{1,0:T(8,128)(2,1)S(1)} all-gather(bf16[16,768]{1,0:T(8,128)(2,1)S(1)} %copy-done.5), channel_id=1, replica_groups={{0,128,256,384},{8,136,264,392},{16,144,272,400},{24,152,280,408},{32,1..., dimensions={0}, use_global_device_ids=true | all-gather | bytes 122880 | tf_op jit(solution)/shard_map/all_gather | solution.py:49
  45.9 0.9 gather_fusion
  46.7 0.7 reshape.51
  47.5 9.0 %all-to-all-start.1 = ((bf16[64,2,640]{2,1,0:T(2,128)(2,1)}), bf16[64,2,640]{2,1,0:T(2,128)(2,1)S(1)}, u32[]{:S(2)}, u32[]{:S(2)}) async-start(bf16[64,2,640]{2,1,0:T(2,128)(2,1)} %reshape.51), calls=%async_computation.1 | async-start | bytes 327680 | tf_op jit(solution)/shard_map/all_to_all | solution.py:43
  56.5 3.4 %collective-permute-start = (bf16[64,768]{1,0:T(8,128)(2,1)S(1)}, bf16[64,768]{1,0:T(8,128)(2,1)S(1)}, u32[]{:S(2)}, u32[]{:S(2)}) collective-permute-start(bf16[64,768]{1,0:T(8,128)(2,1)S(1)} %all_gather.9), channel_id=1, source_target_pairs={{0,16},{8,24},{16,0},{24,8},{32,48},{40,56},{48,32},{56,40},{64,80... | collective-permute-start | bytes 294920 | tf_op jit(solution)/shard_map/ppermute | solution.py:39
  59.9 3.8 %collective-permute-done = bf16[64,768]{1,0:T(8,128)(2,1)S(1)} collective-permute-done((bf16[64,768]{1,0:T(8,128)(2,1)S(1)}, bf16[64,768]{1,0:T(8,128)(2,1)S(1)}, u32[]{:S(2)}, u32[]{:S(2)}) %collective-permute-start) | collective-permute-done | bytes 98336 | tf_op jit(solution)/shard_map/ppermute | solution.py:39
  63.7 17.9 %all_gather.10 = bf16[512,768]{1,0:T(8,128)(2,1)S(1)} all-gather(bf16[128,768]{1,0:T(8,128)(2,1)S(1)} %pad_maximum_fusion), channel_id=1, replica_groups={{0,32,64,96},{8,40,72,104},{16,48,80,112},{24,56,88,120},{128,160,192,2..., dimensions={0}, use_global_device_ids=true | all-gather | bytes 983040 | tf_op jit(solution)/shard_map/all_gather | solution.py:49
  81.6 0.7 copy.22
  82.3 2.1 order_rows.1
  84.4 6.8 %all-to-all-start.2 = ((bf16[8,640,128]{2,1,0:T(8,128)(2,1)}), bf16[8,640,128]{2,1,0:T(8,128)(2,1)S(1)}, u32[]{:S(2)}, u32[]{:S(2)}) async-start(bf16[8,640,128]{2,1,0:T(8,128)(2,1)} %order_rows.1), calls=%async_computation.2 | async-start | bytes 2621440 | tf_op jit(solution)/shard_map/all_to_all | solution.py:43
  91.2 1.9 collective-permute-start.1
  93.2 0.6 reshape.53.gain_ref
  93.8 0.6 pad_add_fusion.place_ref
  94.4 1.0 collective-permute-done.1.core_ref
  95.4 13.2 %all-to-all-done.2.gathered_ref = bf16[8,640,128]{2,1,0:T(8,128)(2,1)S(1)} async-done(((bf16[8,640,128]{2,1,0:T(8,128)(2,1)}), bf16[8,640,128]{2,1,0:T(8,128)(2,1)S(1)}, u32[]{:S(2)}, u32[]{:S(2)}) %all-to-all-start.2) | async-done | bytes 1310752 | tf_op jit(solution)/shard_map/all_to_all | solution.py:43
  108.6 1.1 copy-done
  109.7 5.2 %forward.1 = (bf16[8,640,128]{2,1,0:T(8,128)(2,1)}, f32[512,768]{1,0:T(8,128)}, bf16[512,1024]{1,0:T(8,128)(2,1)}) custom-call(s32[2]{0:T(128)} %pad_add_fusion.place_ref, bf16[8,640,128]{2,1,0:T(8,128)(2,1)} %copy-done, bf16[4,2,4,16,768]{4,3,2,1,0:T(8,128)(2,1)} %bitcast.37, bf16[4,2,4,16,768]{4,3,2,1,0:T(8,128)(2,1)} %copy-done.4, ...), custom_call_target="tpu_custom_call" | custom-call | tf_op jit(solution)/shard_map/forward/pallas_call | solution.py:314
  114.9 3.7 %all-to-all-start.3 = ((bf16[8,640,128]{2,1,0:T(8,128)(2,1)}), bf16[8,640,128]{2,1,0:T(8,128)(2,1)S(1)}, u32[]{:S(2)}, u32[]{:S(2)}) async-start(bf16[8,640,128]{2,1,0:T(8,128)(2,1)} %get-tuple-element.28), calls=%async_computation.3 | async-start | bytes 2621440 | tf_op jit(solution)/shard_map/all_to_all | solution.py:43
  118.6 1.3 copy.19
  119.9 1.6 slice.23.labels_ref
  121.5 14.3 %all-to-all-done.3.sent_ref = bf16[8,640,128]{2,1,0:T(8,128)(2,1)S(1)} async-done(((bf16[8,640,128]{2,1,0:T(8,128)(2,1)}), bf16[8,640,128]{2,1,0:T(8,128)(2,1)S(1)}, u32[]{:S(2)}, u32[]{:S(2)}) %all-to-all-start.3) | async-done | bytes 1310752 | tf_op jit(solution)/shard_map/all_to_all | solution.py:43
  135.8 1.1 copy-done.1
  136.8 5.2 %backward.1 = (bf16[512,768]{1,0:T(8,128)(2,1)}, bf16[512,768]{1,0:T(8,128)(2,1)}, bf16[128,896]{1,0:T(8,128)(2,1)}) custom-call(bf16[8,640,128]{2,1,0:T(8,128)(2,1)} %copy-done.1, bf16[8,64,128]{2,1,0:T(8,128)(2,1)} %slice.23.labels_ref, f32[512,768]{1,0:T(8,128)} %get-tuple-element.29.hidden_ref, f32[1,768]{1,0:T(1,128)} %reshape.53.gain_ref, ...), custom_call_target="tpu_custom_call" | custom-call | tf_op jit(solution)/shard_map/backward/pallas_call | solution.py:314
  142.0 3.6 %weight.1 = (f32[512,768]{1,0:T(8,128)}, bf16[512,768]{1,0:T(8,128)(2,1)}) custom-call(s32[2]{0:T(128)} %pad_add_fusion.place_ref, bf16[1024,512]{1,0:T(8,128)(2,1)} %bitcast.35, bf16[512,768]{1,0:T(8,128)(2,1)} %get-tuple-element.32.back_ref), custom_call_target="tpu_custom_call" | custom-call | tf_op jit(solution)/shard_map/weight/pallas_call | solution.py:314
  145.6 1.9 collective-permute-start.2
  147.5 2.5 %collective-permute-done.2 = bf16[512,768]{1,0:T(8,128)(2,1)S(1)} collective-permute-done((bf16[512,768]{1,0:T(8,128)(2,1)}, bf16[512,768]{1,0:T(8,128)(2,1)S(1)}, u32[]{:S(2)}, u32[]{:S(2)}) %collective-permute-start.2) | collective-permute-done | bytes 786464 | tf_op jit(solution)/shard_map/ppermute | solution.py:39
  150.0 1.6 convert_add_fusion
  151.7 3.1 %collective-permute-start.3 = (bf16[256,768]{1,0:T(8,128)(2,1)S(1)}, bf16[256,768]{1,0:T(8,128)(2,1)S(1)}, u32[]{:S(2)}, u32[]{:S(2)}) collective-permute-start(bf16[256,768]{1,0:T(8,128)(2,1)S(1)} %slice.31), channel_id=1, source_target_pairs={{0,16},{8,24},{16,0},{24,8},{32,48},{40,56},{48,32},{56,40},{64,80... | collective-permute-start | bytes 1179656 | tf_op jit(solution)/shard_map/ppermute | solution.py:39
  154.8 11.4 %all-to-all-start.4 = ((bf16[16,8,896]{2,1,0:T(8,128)(2,1)}), bf16[16,8,896]{2,1,0:T(8,128)(2,1)S(1)}, u32[]{:S(2)}, u32[]{:S(2)}) async-start(bf16[16,8,896]{2,1,0:T(8,128)(2,1)} %bitcast.13), calls=%async_computation.4 | async-start | bytes 458752 | tf_op jit(solution)/shard_map/all_to_all | solution.py:43
  166.2 0.1 convert_add_fusion.1
  166.3 3.4 %collective-permute-start.4 = (bf16[64,768]{1,0:T(8,128)(2,1)S(1)}, bf16[64,768]{1,0:T(8,128)(2,1)S(1)}, u32[]{:S(2)}, u32[]{:S(2)}) collective-permute-start(bf16[64,768]{1,0:T(8,128)(2,1)S(1)} %get-tuple-element.48), channel_id=1, source_target_pairs={{0,32},{8,40},{16,48},{24,56},{32,64},{40,72},{48,80},{56,88},{64,... | collective-permute-start | bytes 294920 | tf_op jit(solution)/shard_map/ppermute | solution.py:39
  169.7 2.5 %collective-permute-start.6 = (bf16[64,768]{1,0:T(8,128)(2,1)S(1)}, bf16[64,768]{1,0:T(8,128)(2,1)S(1)}, u32[]{:S(2)}, u32[]{:S(2)}) collective-permute-start(bf16[64,768]{1,0:T(8,128)(2,1)S(1)} %get-tuple-element.49), channel_id=1, source_target_pairs={{0,96},{8,104},{16,112},{24,120},{32,0},{40,8},{48,16},{56,24},{64... | collective-permute-start | bytes 294920 | tf_op jit(solution)/shard_map/ppermute | solution.py:39
  172.2 4.3 %collective-permute-start.5 = (bf16[64,768]{1,0:T(8,128)(2,1)S(1)}, bf16[64,768]{1,0:T(8,128)(2,1)S(1)}, u32[]{:S(2)}, u32[]{:S(2)}) collective-permute-start(bf16[64,768]{1,0:T(8,128)(2,1)S(1)} %get-tuple-element.50), channel_id=1, source_target_pairs={{0,64},{8,72},{16,80},{24,88},{32,96},{40,104},{48,112},{56,120},{... | collective-permute-start | bytes 294920 | tf_op jit(solution)/shard_map/ppermute | solution.py:39
  176.4 1.6 collective-permute-done.4
  178.1 5.5 %all-to-all-done.4 = bf16[16,8,896]{2,1,0:T(8,128)(2,1)S(1)} async-done(((bf16[16,8,896]{2,1,0:T(8,128)(2,1)}), bf16[16,8,896]{2,1,0:T(8,128)(2,1)S(1)}, u32[]{:S(2)}, u32[]{:S(2)}) %all-to-all-start.4) | async-done | bytes 229408 | tf_op jit(solution)/shard_map/all_to_all | solution.py:43
  183.6 1.9 collective-permute-start.7
  185.6 1.2 collective-permute-done.7
  186.7 3.4 %collective-permute-start.8 = (f32[8,896]{1,0:T(8,128)S(1)}, f32[8,896]{1,0:T(8,128)S(1)}, u32[]{:S(2)}, u32[]{:S(2)}) collective-permute-start(f32[8,896]{1,0:T(8,128)S(1)} %add.90), channel_id=1, source_target_pairs={{0,16},{8,24},{16,0},{24,8},{32,48},{40,56},{48,32},{56,40},{64,80... | collective-permute-start | bytes 86024 | tf_op jit(solution)/shard_map/ppermute | solution.py:39
  190.1 0.7 fusion.2
  190.8 7.3 %all-to-all-start.5 = ((bf16[4,16,768]{2,1,0:T(8,128)(2,1)}), bf16[4,16,768]{2,1,0:T(8,128)(2,1)S(1)}, u32[]{:S(2)}, u32[]{:S(2)}) async-start(bf16[4,16,768]{2,1,0:T(8,128)(2,1)} %bitcast.17), calls=%async_computation.5 | async-start | bytes 196608 | tf_op jit(solution)/shard_map/all_to_all | solution.py:43
  198.2 37.0 %all_gather.11 = f32[128,896]{1,0:T(8,128)S(1)} all-gather(f32[8,896]{1,0:T(8,128)S(1)} %add.91), channel_id=1, replica_groups={{0,32,64,96,128,160,192,224,256,288,320,352,384,416,448,480},{8,40,72,1..., dimensions={0}, use_global_device_ids=true | all-gather | bytes 487424 | tf_op jit(solution)/shard_map/all_gather | solution.py:49
  235.2 0.9 copy.20
  236.1 0.7 reshape_squeeze.3
  236.8 0.6 convert_reduce_fusion.1
  (32 shorter events, 0.3 us)
Async XLA Ops:
  0.6 45.1 %copy-start.7 = (s32[128]{0:T(128)S(1)}, s32[128]{0:T(128)}, u32[]{:S(2)}) copy-start(s32[128]{0:T(128)} %param.10) | copy-start | bytes 1540
  0.6 21.8 %copy-start.5 = (bf16[16,768]{1,0:T(8,128)(2,1)S(1)}, bf16[16,768]{1,0:T(8,128)(2,1)}, u32[]{:S(2)}) copy-start(bf16[16,768]{1,0:T(8,128)(2,1)} %param.13) | copy-start | bytes 73732
  5.8 40.0 %all-to-all-start = ((bf16[64,2,640]{2,1,0:T(2,128)(2,1)}), bf16[64,2,640]{2,1,0:T(2,128)(2,1)S(1)}, u32[]{:S(2)}, u32[]{:S(2)}) async-start(bf16[64,2,640]{2,1,0:T(2,128)(2,1)} %copy.17), calls=%async_computation | async-start | bytes 327680 | tf_op jit(solution)/shard_map/all_to_all | solution.py:43
  47.5 34.1 %all-to-all-start.1 = ((bf16[64,2,640]{2,1,0:T(2,128)(2,1)}), bf16[64,2,640]{2,1,0:T(2,128)(2,1)S(1)}, u32[]{:S(2)}, u32[]{:S(2)}) async-start(bf16[64,2,640]{2,1,0:T(2,128)(2,1)} %reshape.51), calls=%async_computation.1 | async-start | bytes 327680 | tf_op jit(solution)/shard_map/all_to_all | solution.py:43
  56.5 7.2 %collective-permute-start = (bf16[64,768]{1,0:T(8,128)(2,1)S(1)}, bf16[64,768]{1,0:T(8,128)(2,1)S(1)}, u32[]{:S(2)}, u32[]{:S(2)}) collective-permute-start(bf16[64,768]{1,0:T(8,128)(2,1)S(1)} %all_gather.9), channel_id=1, source_target_pairs={{0,16},{8,24},{16,0},{24,8},{32,48},{40,56},{48,32},{56,40},{64,80... | collective-permute-start | bytes 294920 | tf_op jit(solution)/shard_map/ppermute | solution.py:39
  81.6 9.6 %copy-start.2 = (bf16[512,768]{1,0:T(8,128)(2,1)}, bf16[512,768]{1,0:T(8,128)(2,1)S(1)}, u32[]{:S(2)}) copy-start(bf16[512,768]{1,0:T(8,128)(2,1)S(1)} %all_gather.10) | copy-start | bytes 2359300
  84.4 8.7 %copy-start.6 = (f32[768]{0:T(1024)S(1)}, f32[768]{0:T(1024)}, u32[]{:S(2)}) copy-start(f32[768]{0:T(1024)} %param.14) | copy-start | bytes 9220
  84.4 24.2 %all-to-all-start.2 = ((bf16[8,640,128]{2,1,0:T(8,128)(2,1)}), bf16[8,640,128]{2,1,0:T(8,128)(2,1)S(1)}, u32[]{:S(2)}, u32[]{:S(2)}) async-start(bf16[8,640,128]{2,1,0:T(8,128)(2,1)} %order_rows.1), calls=%async_computation.2 | async-start | bytes 2621440 | tf_op jit(solution)/shard_map/all_to_all | solution.py:43
  91.2 4.2 %collective-permute-start.1 = (bf16[4,2,4,16,768]{4,3,2,1,0:T(8,128)(2,1)S(1)}, bf16[4,2,4,16,768]{4,3,2,1,0:T(8,128)(2,1)S(1)}, u32[]{:S(2)}, u32[]{:S(2)}) collective-permute-start(bf16[4,2,4,16,768]{4,3,2,1,0:T(8,128)(2,1)S(1)} %bitcast.36), channel_id=1, source_target_pairs={{0,8},{8,0},{16,24},{24,16},{32,40},{40,32},{48,56},{56,48},{64,72... | collective-permute-start | bytes 2359304 | tf_op jit(solution)/shard_map/ppermute | solution.py:39
  95.4 13.2 %copy-start.4 = (bf16[4,2,4,16,768]{4,3,2,1,0:T(8,128)(2,1)}, bf16[4,2,4,16,768]{4,3,2,1,0:T(8,128)(2,1)S(1)}, u32[]{:S(2)}) copy-start(bf16[4,2,4,16,768]{4,3,2,1,0:T(8,128)(2,1)S(1)} %collective-permute-done.1.core_ref) | copy-start | bytes 2359300
  108.6 1.1 copy-start
  114.9 3.7 %copy-start.3 = (bf16[512,1024]{1,0:T(8,128)(2,1)S(1)}, bf16[512,1024]{1,0:T(8,128)(2,1)}, u32[]{:S(2)}) copy-start(bf16[512,1024]{1,0:T(8,128)(2,1)} %get-tuple-element.31) | copy-start | bytes 3145732
  114.9 20.9 %all-to-all-start.3 = ((bf16[8,640,128]{2,1,0:T(8,128)(2,1)}), bf16[8,640,128]{2,1,0:T(8,128)(2,1)S(1)}, u32[]{:S(2)}, u32[]{:S(2)}) async-start(bf16[8,640,128]{2,1,0:T(8,128)(2,1)} %get-tuple-element.28), calls=%async_computation.3 | async-start | bytes 2621440 | tf_op jit(solution)/shard_map/all_to_all | solution.py:43
  135.8 1.1 copy-start.1
  145.6 4.4 %collective-permute-start.2 = (bf16[512,768]{1,0:T(8,128)(2,1)}, bf16[512,768]{1,0:T(8,128)(2,1)S(1)}, u32[]{:S(2)}, u32[]{:S(2)}) collective-permute-start(bf16[512,768]{1,0:T(8,128)(2,1)} %get-tuple-element.34), channel_id=1, source_target_pairs={{0,8},{8,0},{16,24},{24,16},{32,40},{40,32},{48,56},{56,48},{64,72... | collective-permute-start | bytes 2359304 | tf_op jit(solution)/shard_map/ppermute | solution.py:39
  151.7 14.5 %collective-permute-start.3 = (bf16[256,768]{1,0:T(8,128)(2,1)S(1)}, bf16[256,768]{1,0:T(8,128)(2,1)S(1)}, u32[]{:S(2)}, u32[]{:S(2)}) collective-permute-start(bf16[256,768]{1,0:T(8,128)(2,1)S(1)} %slice.31), channel_id=1, source_target_pairs={{0,16},{8,24},{16,0},{24,8},{32,48},{40,56},{48,32},{56,40},{64,80... | collective-permute-start | bytes 1179656 | tf_op jit(solution)/shard_map/ppermute | solution.py:39
  154.8 28.8 %all-to-all-start.4 = ((bf16[16,8,896]{2,1,0:T(8,128)(2,1)}), bf16[16,8,896]{2,1,0:T(8,128)(2,1)S(1)}, u32[]{:S(2)}, u32[]{:S(2)}) async-start(bf16[16,8,896]{2,1,0:T(8,128)(2,1)} %bitcast.13), calls=%async_computation.4 | async-start | bytes 458752 | tf_op jit(solution)/shard_map/all_to_all | solution.py:43
  166.3 11.8 %collective-permute-start.4 = (bf16[64,768]{1,0:T(8,128)(2,1)S(1)}, bf16[64,768]{1,0:T(8,128)(2,1)S(1)}, u32[]{:S(2)}, u32[]{:S(2)}) collective-permute-start(bf16[64,768]{1,0:T(8,128)(2,1)S(1)} %get-tuple-element.48), channel_id=1, source_target_pairs={{0,32},{8,40},{16,48},{24,56},{32,64},{40,72},{48,80},{56,88},{64,... | collective-permute-start | bytes 294920 | tf_op jit(solution)/shard_map/ppermute | solution.py:39
  169.7 20.4 %collective-permute-start.6 = (bf16[64,768]{1,0:T(8,128)(2,1)S(1)}, bf16[64,768]{1,0:T(8,128)(2,1)S(1)}, u32[]{:S(2)}, u32[]{:S(2)}) collective-permute-start(bf16[64,768]{1,0:T(8,128)(2,1)S(1)} %get-tuple-element.49), channel_id=1, source_target_pairs={{0,96},{8,104},{16,112},{24,120},{32,0},{40,8},{48,16},{56,24},{64... | collective-permute-start | bytes 294920 | tf_op jit(solution)/shard_map/ppermute | solution.py:39
  172.2 18.0 %collective-permute-start.5 = (bf16[64,768]{1,0:T(8,128)(2,1)S(1)}, bf16[64,768]{1,0:T(8,128)(2,1)S(1)}, u32[]{:S(2)}, u32[]{:S(2)}) collective-permute-start(bf16[64,768]{1,0:T(8,128)(2,1)S(1)} %get-tuple-element.50), channel_id=1, source_target_pairs={{0,64},{8,72},{16,80},{24,88},{32,96},{40,104},{48,112},{56,120},{... | collective-permute-start | bytes 294920 | tf_op jit(solution)/shard_map/ppermute | solution.py:39
  183.6 3.1 %collective-permute-start.7 = (f32[8,896]{1,0:T(8,128)S(1)}, f32[8,896]{1,0:T(8,128)S(1)}, u32[]{:S(2)}, u32[]{:S(2)}) collective-permute-start(f32[8,896]{1,0:T(8,128)S(1)} %convert_reduce_fusion), channel_id=1, source_target_pairs={{0,8},{8,0},{16,24},{24,16},{32,40},{40,32},{48,56},{56,48},{64,72... | collective-permute-start | bytes 86024 | tf_op jit(solution)/shard_map/ppermute | solution.py:39
  186.7 11.4 %collective-permute-start.8 = (f32[8,896]{1,0:T(8,128)S(1)}, f32[8,896]{1,0:T(8,128)S(1)}, u32[]{:S(2)}, u32[]{:S(2)}) collective-permute-start(f32[8,896]{1,0:T(8,128)S(1)} %add.90), channel_id=1, source_target_pairs={{0,16},{8,24},{16,0},{24,8},{32,48},{40,56},{48,32},{56,40},{64,80... | collective-permute-start | bytes 86024 | tf_op jit(solution)/shard_map/ppermute | solution.py:39
  190.8 45.9 %all-to-all-start.5 = ((bf16[4,16,768]{2,1,0:T(8,128)(2,1)}), bf16[4,16,768]{2,1,0:T(8,128)(2,1)S(1)}, u32[]{:S(2)}, u32[]{:S(2)}) async-start(bf16[4,16,768]{2,1,0:T(8,128)(2,1)} %bitcast.17), calls=%async_computation.5 | async-start | bytes 196608 | tf_op jit(solution)/shard_map/all_to_all | solution.py:43

commit v4 on v3

--- a/solution.py
+++ b/solution.py
@@ -296,7 +296,7 @@
             for zl in range(4):
                 for zh in range(4):
                     block = ((zh * 4 + zl) * 2 + (xl ^ dx)) * 2 + (c ^ dc)
-                    row = dx * 256 + (zl * 4 + zh) * 16
+                    row = dx * 256 + (zh * 4 + zl) * 16
                     held[dc, row : row + 16, :] = turned_ref[
                         pl.ds(pl.multiple_of(block * 16, 16), 16), :
                     ]
@@ -379,17 +379,12 @@
     head_rows, kept = tie(head_rows, kept)
     part = exchange(head_rows.reshape(16, 8, 896), "dp", Z_GROUPS)
     kept = kept[:256] + permute(kept[256:].astype(BF), to_xlo).astype(F32)
-    blocks = kept.reshape(4, 64, 768)
-    from_zl = [permute(take(blocks, (zl + k) % 4, 0).astype(BF), to_zl(k)) for k in (1, 2, 3)]
-    part, first = tie(part, from_zl[0])
+    part, kept = tie(part, kept)
+    grad_proj = exchange(kept.astype(BF).reshape(16, 16, 768), "dp", Z_GROUPS)
+    grad_proj = jnp.sum(grad_proj.astype(F32), axis=0)
     part = jnp.sum(part.astype(F32), axis=0)
     part = part + permute(part, to_core)
-    kept = take(blocks, zl, 0)
-    for block in (first, from_zl[1], from_zl[2]):
-        kept = kept + block.astype(F32)
     part = part + permute(part, to_xlo)
-    grad_proj = exchange(kept.astype(BF).reshape(4, 16, 768), "dp", ZH_GROUPS)
-    grad_proj = jnp.sum(grad_proj.astype(F32), axis=0)
     whole = gather(part, "dp", Z_GROUPS).reshape(16, 8, 896)
     grad_head = jnp.transpose(whole[:, :, :768].reshape(128, 768))
     grad_gain = whole[:, 0, 768:816].reshape(768)

time: 238 us -> 236 us (level)
  the two profiles are of different devices: /device:TPU:32 before, /device:TPU:2 now
where the time goes in v4:
time: 236 us; the launch traced here: 235 us
  blocking collectives  78.7 us (33%)
  starting transfers between devices  69.3 us (29%)
  waiting for transfers between devices  51.2 us (22%)
  Pallas kernels  18.7 us (8%)
  local copies, waits for them, and re-layouts  11.5 us (5%)
  other arithmetic  4.43 us (2%)
    all_gather x3, blocking collectives, gather(): return lax.all_gather(x, axis, axis=0, tiled=True, axis_index_groups=groups)  78.7 us
    all_to_all x6, starting transfers between devices, exchange(): lax.all_to_all(x, axis, split_axis=0, concat_axis=0, tiled=True, axis_ind...  54.4 us
    all_to_all x6, waiting for transfers between devices, exchange(): lax.all_to_all(x, axis, split_axis=0, concat_axis=0, tiled=True, axis_ind...  30 us
    ppermute x6, waiting for transfers between devices, permute(): return lax.ppermute(x, 'dp', [(i, target(i)) for i in range(N_DP)])  21.2 us
    ppermute x6, starting transfers between devices, permute(): return lax.ppermute(x, 'dp', [(i, target(i)) for i in range(N_DP)])  14.9 us
    pallas_call x3, Pallas kernels, call(): pl.pallas_call(kernel, out_shape=outs, in_specs=specs, out_specs=jax.tree...  13.8 us
  transfers between devices with their start and end apart: 12, of which 9 were waited for; matrix products, arithmetic and copies ran while one was open for 3% of the time, Pallas kernels for 0%

profile of v4, /device:TPU:2, one launch (start us, length us, event | category | flops | bytes accessed | tf_op | source)
XLA Modules:
  0.0 234.6 jit_solution(14630768755698627942)
XLA Ops:
  0.6 0.0 copy-start.7
  0.7 0.6 pad_add_fusion.1.position_ref
  1.2 2.8 %cut_windows.1 = bf16[2,64,640]{2,1,0:T(8,128)(2,1)} custom-call(s32[2]{0:T(128)} %pad_add_fusion.1.position_ref, s32[1,128]{1,0:T(1,128)} %bitcast.29, s32[1,128]{1,0:T(1,128)} %bitcast.27, s32[1,128]{1,0:T(1,128)} %bitcast.28, bf16[8,512,128]{2,1,0:T(8,128)(2,1)} %latents_ref.1, bf16[8,512,128]{2,1,0:T(8,128)(2,1)} %labels_ref.1), custom_call_target="tpu_custom_call" | custom-call | tf_op jit(solution)/shard_map/cut_windows/pallas_call | solution.py:106
  4.0 1.8 copy.17
  5.8 17.1 %all-to-all-start = ((bf16[64,2,640]{2,1,0:T(2,128)(2,1)}), bf16[64,2,640]{2,1,0:T(2,128)(2,1)S(1)}, u32[]{:S(2)}, u32[]{:S(2)}) async-start(bf16[64,2,640]{2,1,0:T(2,128)(2,1)} %copy.17), calls=%async_computation | async-start | bytes 327680 | tf_op jit(solution)/shard_map/all_to_all | solution.py:43
  22.9 23.6 %all_gather.9 = bf16[64,768]{1,0:T(8,128)(2,1)S(1)} all-gather(bf16[16,768]{1,0:T(8,128)(2,1)S(1)} %copy-done.5), channel_id=1, replica_groups={{0,128,256,384},{8,136,264,392},{16,144,272,400},{24,152,280,408},{32,1..., dimensions={0}, use_global_device_ids=true | all-gather | bytes 122880 | tf_op jit(solution)/shard_map/all_gather | solution.py:49
  46.5 0.0 all-to-all-done
  46.5 0.1 reshape.44
  46.5 0.9 gather_fusion
  47.4 0.7 reshape.45
  48.2 8.8 %all-to-all-start.1 = ((bf16[64,2,640]{2,1,0:T(2,128)(2,1)}), bf16[64,2,640]{2,1,0:T(2,128)(2,1)S(1)}, u32[]{:S(2)}, u32[]{:S(2)}) async-start(bf16[64,2,640]{2,1,0:T(2,128)(2,1)} %reshape.45), calls=%async_computation.1 | async-start | bytes 327680 | tf_op jit(solution)/shard_map/all_to_all | solution.py:43
  56.9 2.4 %collective-permute-start = (bf16[64,768]{1,0:T(8,128)(2,1)S(1)}, bf16[64,768]{1,0:T(8,128)(2,1)S(1)}, u32[]{:S(2)}, u32[]{:S(2)}) collective-permute-start(bf16[64,768]{1,0:T(8,128)(2,1)S(1)} %all_gather.9), channel_id=1, source_target_pairs={{0,16},{8,24},{16,0},{24,8},{32,48},{40,56},{48,32},{56,40},{64,80... | collective-permute-start | bytes 294920 | tf_op jit(solution)/shard_map/ppermute | solution.py:39
  59.3 4.8 %collective-permute-done = bf16[64,768]{1,0:T(8,128)(2,1)S(1)} collective-permute-done((bf16[64,768]{1,0:T(8,128)(2,1)S(1)}, bf16[64,768]{1,0:T(8,128)(2,1)S(1)}, u32[]{:S(2)}, u32[]{:S(2)}) %collective-permute-start) | collective-permute-done | bytes 98336 | tf_op jit(solution)/shard_map/ppermute | solution.py:39
  64.2 19.7 %all_gather.10 = bf16[512,768]{1,0:T(8,128)(2,1)S(1)} all-gather(bf16[128,768]{1,0:T(8,128)(2,1)S(1)} %pad_maximum_fusion), channel_id=1, replica_groups={{0,32,64,96},{8,40,72,104},{16,48,80,112},{24,56,88,120},{128,160,192,2..., dimensions={0}, use_global_device_ids=true | all-gather | bytes 983040 | tf_op jit(solution)/shard_map/all_gather | solution.py:49
  83.9 0.7 copy.22
  84.6 2.1 order_rows.1
  86.8 6.2 %all-to-all-start.2 = ((bf16[8,640,128]{2,1,0:T(8,128)(2,1)}), bf16[8,640,128]{2,1,0:T(8,128)(2,1)S(1)}, u32[]{:S(2)}, u32[]{:S(2)}) async-start(bf16[8,640,128]{2,1,0:T(8,128)(2,1)} %order_rows.1), calls=%async_computation.2 | async-start | bytes 2621440 | tf_op jit(solution)/shard_map/all_to_all | solution.py:43
  92.9 1.9 collective-permute-start.1
  94.9 0.6 reshape.47.gain_ref
  95.5 0.7 pad_add_fusion.place_ref
  96.1 1.0 collective-permute-done.1.core_ref
  97.1 12.3 %all-to-all-done.2.gathered_ref = bf16[8,640,128]{2,1,0:T(8,128)(2,1)S(1)} async-done(((bf16[8,640,128]{2,1,0:T(8,128)(2,1)}), bf16[8,640,128]{2,1,0:T(8,128)(2,1)S(1)}, u32[]{:S(2)}, u32[]{:S(2)}) %all-to-all-start.2) | async-done | bytes 1310752 | tf_op jit(solution)/shard_map/all_to_all | solution.py:43
  109.4 1.1 copy-done
  110.5 5.1 %forward.1 = (bf16[8,640,128]{2,1,0:T(8,128)(2,1)}, f32[512,768]{1,0:T(8,128)}, bf16[512,1024]{1,0:T(8,128)(2,1)}) custom-call(s32[2]{0:T(128)} %pad_add_fusion.place_ref, bf16[8,640,128]{2,1,0:T(8,128)(2,1)} %copy-done, bf16[4,2,4,16,768]{4,3,2,1,0:T(8,128)(2,1)} %bitcast.22, bf16[4,2,4,16,768]{4,3,2,1,0:T(8,128)(2,1)} %copy-done.4, ...), custom_call_target="tpu_custom_call" | custom-call | tf_op jit(solution)/shard_map/forward/pallas_call | solution.py:314
  115.5 3.7 %all-to-all-start.3 = ((bf16[8,640,128]{2,1,0:T(8,128)(2,1)}), bf16[8,640,128]{2,1,0:T(8,128)(2,1)S(1)}, u32[]{:S(2)}, u32[]{:S(2)}) async-start(bf16[8,640,128]{2,1,0:T(8,128)(2,1)} %get-tuple-element.28), calls=%async_computation.3 | async-start | bytes 2621440 | tf_op jit(solution)/shard_map/all_to_all | solution.py:43
  119.2 1.3 copy.19
  120.6 1.6 slice.23.labels_ref
  122.1 14.3 %all-to-all-done.3.sent_ref = bf16[8,640,128]{2,1,0:T(8,128)(2,1)S(1)} async-done(((bf16[8,640,128]{2,1,0:T(8,128)(2,1)}), bf16[8,640,128]{2,1,0:T(8,128)(2,1)S(1)}, u32[]{:S(2)}, u32[]{:S(2)}) %all-to-all-start.3) | async-done | bytes 1310752 | tf_op jit(solution)/shard_map/all_to_all | solution.py:43
  136.4 1.1 copy-done.1
  137.5 5.2 %backward.1 = (bf16[512,768]{1,0:T(8,128)(2,1)}, bf16[512,768]{1,0:T(8,128)(2,1)}, bf16[128,896]{1,0:T(8,128)(2,1)}) custom-call(bf16[8,640,128]{2,1,0:T(8,128)(2,1)} %copy-done.1, bf16[8,64,128]{2,1,0:T(8,128)(2,1)} %slice.23.labels_ref, f32[512,768]{1,0:T(8,128)} %get-tuple-element.29.hidden_ref, f32[1,768]{1,0:T(1,128)} %reshape.47.gain_ref, ...), custom_call_target="tpu_custom_call" | custom-call | tf_op jit(solution)/shard_map/backward/pallas_call | solution.py:314
  142.7 3.6 %weight.1 = (f32[512,768]{1,0:T(8,128)}, bf16[512,768]{1,0:T(8,128)(2,1)}) custom-call(s32[2]{0:T(128)} %pad_add_fusion.place_ref, bf16[1024,512]{1,0:T(8,128)(2,1)} %bitcast.20, bf16[512,768]{1,0:T(8,128)(2,1)} %get-tuple-element.32.back_ref), custom_call_target="tpu_custom_call" | custom-call | tf_op jit(solution)/shard_map/weight/pallas_call | solution.py:314
  146.3 1.9 collective-permute-start.2
  148.2 2.5 %collective-permute-done.2 = bf16[512,768]{1,0:T(8,128)(2,1)S(1)} collective-permute-done((bf16[512,768]{1,0:T(8,128)(2,1)}, bf16[512,768]{1,0:T(8,128)(2,1)S(1)}, u32[]{:S(2)}, u32[]{:S(2)}) %collective-permute-start.2) | collective-permute-done | bytes 786464 | tf_op jit(solution)/shard_map/ppermute | solution.py:39
  150.6 1.6 convert_add_fusion
  152.2 10.4 %all-to-all-start.4 = ((bf16[16,8,896]{2,1,0:T(8,128)(2,1)}), bf16[16,8,896]{2,1,0:T(8,128)(2,1)S(1)}, u32[]{:S(2)}, u32[]{:S(2)}) async-start(bf16[16,8,896]{2,1,0:T(8,128)(2,1)} %bitcast.11), calls=%async_computation.4 | async-start | bytes 458752 | tf_op jit(solution)/shard_map/all_to_all | solution.py:43
  162.7 3.4 %collective-permute-start.3 = (bf16[256,768]{1,0:T(8,128)(2,1)S(1)}, bf16[256,768]{1,0:T(8,128)(2,1)S(1)}, u32[]{:S(2)}, u32[]{:S(2)}) collective-permute-start(bf16[256,768]{1,0:T(8,128)(2,1)S(1)} %slice.31), channel_id=1, source_target_pairs={{0,16},{8,24},{16,0},{24,8},{32,48},{40,56},{48,32},{56,40},{64,80... | collective-permute-start | bytes 1179656 | tf_op jit(solution)/shard_map/ppermute | solution.py:39
  166.1 9.4 %collective-permute-done.3 = bf16[256,768]{1,0:T(8,128)(2,1)S(1)} collective-permute-done((bf16[256,768]{1,0:T(8,128)(2,1)S(1)}, bf16[256,768]{1,0:T(8,128)(2,1)S(1)}, u32[]{:S(2)}, u32[]{:S(2)}) %collective-permute-start.3) | collective-permute-done | bytes 393248 | tf_op jit(solution)/shard_map/ppermute | solution.py:39
  175.4 0.8 convert_add_fusion.1
  176.3 3.5 %all-to-all-done.4 = bf16[16,8,896]{2,1,0:T(8,128)(2,1)S(1)} async-done(((bf16[16,8,896]{2,1,0:T(8,128)(2,1)}), bf16[16,8,896]{2,1,0:T(8,128)(2,1)S(1)}, u32[]{:S(2)}, u32[]{:S(2)}) %all-to-all-start.4) | async-done | bytes 229408 | tf_op jit(solution)/shard_map/all_to_all | solution.py:43
  179.7 8.3 %all-to-all-start.5 = ((bf16[16,16,768]{2,1,0:T(8,128)(2,1)}), bf16[16,16,768]{2,1,0:T(8,128)(2,1)S(1)}, u32[]{:S(2)}, u32[]{:S(2)}) async-start(bf16[16,16,768]{2,1,0:T(8,128)(2,1)} %bitcast.12), calls=%async_computation.5 | async-start | bytes 786432 | tf_op jit(solution)/shard_map/all_to_all | solution.py:43
  188.1 1.9 collective-permute-start.4
  190.0 1.2 collective-permute-done.4
  191.2 3.4 %collective-permute-start.5 = (f32[8,896]{1,0:T(8,128)S(1)}, f32[8,896]{1,0:T(8,128)S(1)}, u32[]{:S(2)}, u32[]{:S(2)}) collective-permute-start(f32[8,896]{1,0:T(8,128)S(1)} %add.32), channel_id=1, source_target_pairs={{0,16},{8,24},{16,0},{24,8},{32,48},{40,56},{48,32},{56,40},{64,80... | collective-permute-start | bytes 86024 | tf_op jit(solution)/shard_map/ppermute | solution.py:39
  194.6 2.4 %collective-permute-done.5 = f32[8,896]{1,0:T(8,128)S(1)} collective-permute-done((f32[8,896]{1,0:T(8,128)S(1)}, f32[8,896]{1,0:T(8,128)S(1)}, u32[]{:S(2)}, u32[]{:S(2)}) %collective-permute-start.5) | collective-permute-done | bytes 28704 | tf_op jit(solution)/shard_map/ppermute | solution.py:39
  196.9 35.4 %all_gather.11 = f32[128,896]{1,0:T(8,128)S(1)} all-gather(f32[8,896]{1,0:T(8,128)S(1)} %add.33), channel_id=1, replica_groups={{0,32,64,96,128,160,192,224,256,288,320,352,384,416,448,480},{8,40,72,1..., dimensions={0}, use_global_device_ids=true | all-gather | bytes 487424 | tf_op jit(solution)/shard_map/all_gather | solution.py:49
  232.3 0.9 copy.20
  233.3 0.7 reshape_squeeze.3
  233.9 0.7 convert_reduce_fusion
  (24 shorter events, 0.2 us)
Async XLA Ops:
  0.6 45.8 %copy-start.7 = (s32[128]{0:T(128)S(1)}, s32[128]{0:T(128)}, u32[]{:S(2)}) copy-start(s32[128]{0:T(128)} %param.10) | copy-start | bytes 1540
  0.6 22.2 %copy-start.5 = (bf16[16,768]{1,0:T(8,128)(2,1)S(1)}, bf16[16,768]{1,0:T(8,128)(2,1)}, u32[]{:S(2)}) copy-start(bf16[16,768]{1,0:T(8,128)(2,1)} %param.13) | copy-start | bytes 73732
  5.8 40.7 %all-to-all-start = ((bf16[64,2,640]{2,1,0:T(2,128)(2,1)}), bf16[64,2,640]{2,1,0:T(2,128)(2,1)S(1)}, u32[]{:S(2)}, u32[]{:S(2)}) async-start(bf16[64,2,640]{2,1,0:T(2,128)(2,1)} %copy.17), calls=%async_computation | async-start | bytes 327680 | tf_op jit(solution)/shard_map/all_to_all | solution.py:43
  48.2 35.8 %all-to-all-start.1 = ((bf16[64,2,640]{2,1,0:T(2,128)(2,1)}), bf16[64,2,640]{2,1,0:T(2,128)(2,1)S(1)}, u32[]{:S(2)}, u32[]{:S(2)}) async-start(bf16[64,2,640]{2,1,0:T(2,128)(2,1)} %reshape.45), calls=%async_computation.1 | async-start | bytes 327680 | tf_op jit(solution)/shard_map/all_to_all | solution.py:43
  56.9 7.2 %collective-permute-start = (bf16[64,768]{1,0:T(8,128)(2,1)S(1)}, bf16[64,768]{1,0:T(8,128)(2,1)S(1)}, u32[]{:S(2)}, u32[]{:S(2)}) collective-permute-start(bf16[64,768]{1,0:T(8,128)(2,1)S(1)} %all_gather.9), channel_id=1, source_target_pairs={{0,16},{8,24},{16,0},{24,8},{32,48},{40,56},{48,32},{56,40},{64,80... | collective-permute-start | bytes 294920 | tf_op jit(solution)/shard_map/ppermute | solution.py:39
  83.9 9.0 %copy-start.2 = (bf16[512,768]{1,0:T(8,128)(2,1)}, bf16[512,768]{1,0:T(8,128)(2,1)S(1)}, u32[]{:S(2)}) copy-start(bf16[512,768]{1,0:T(8,128)(2,1)S(1)} %all_gather.10) | copy-start | bytes 2359300
  86.8 8.1 %copy-start.6 = (f32[768]{0:T(1024)S(1)}, f32[768]{0:T(1024)}, u32[]{:S(2)}) copy-start(f32[768]{0:T(1024)} %param.14) | copy-start | bytes 9220
  86.8 22.6 %all-to-all-start.2 = ((bf16[8,640,128]{2,1,0:T(8,128)(2,1)}), bf16[8,640,128]{2,1,0:T(8,128)(2,1)S(1)}, u32[]{:S(2)}, u32[]{:S(2)}) async-start(bf16[8,640,128]{2,1,0:T(8,128)(2,1)} %order_rows.1), calls=%async_computation.2 | async-start | bytes 2621440 | tf_op jit(solution)/shard_map/all_to_all | solution.py:43
  92.9 4.2 %collective-permute-start.1 = (bf16[4,2,4,16,768]{4,3,2,1,0:T(8,128)(2,1)S(1)}, bf16[4,2,4,16,768]{4,3,2,1,0:T(8,128)(2,1)S(1)}, u32[]{:S(2)}, u32[]{:S(2)}) collective-permute-start(bf16[4,2,4,16,768]{4,3,2,1,0:T(8,128)(2,1)S(1)} %bitcast.21), channel_id=1, source_target_pairs={{0,8},{8,0},{16,24},{24,16},{32,40},{40,32},{48,56},{56,48},{64,72... | collective-permute-start | bytes 2359304 | tf_op jit(solution)/shard_map/ppermute | solution.py:39
  97.1 12.3 %copy-start.4 = (bf16[4,2,4,16,768]{4,3,2,1,0:T(8,128)(2,1)}, bf16[4,2,4,16,768]{4,3,2,1,0:T(8,128)(2,1)S(1)}, u32[]{:S(2)}) copy-start(bf16[4,2,4,16,768]{4,3,2,1,0:T(8,128)(2,1)S(1)} %collective-permute-done.1.core_ref) | copy-start | bytes 2359300
  109.4 1.1 copy-start
  115.5 3.7 %copy-start.3 = (bf16[512,1024]{1,0:T(8,128)(2,1)S(1)}, bf16[512,1024]{1,0:T(8,128)(2,1)}, u32[]{:S(2)}) copy-start(bf16[512,1024]{1,0:T(8,128)(2,1)} %get-tuple-element.31) | copy-start | bytes 3145732
  115.5 20.9 %all-to-all-start.3 = ((bf16[8,640,128]{2,1,0:T(8,128)(2,1)}), bf16[8,640,128]{2,1,0:T(8,128)(2,1)S(1)}, u32[]{:S(2)}, u32[]{:S(2)}) async-start(bf16[8,640,128]{2,1,0:T(8,128)(2,1)} %get-tuple-element.28), calls=%async_computation.3 | async-start | bytes 2621440 | tf_op jit(solution)/shard_map/all_to_all | solution.py:43
  136.4 1.1 copy-start.1
  146.3 4.4 %collective-permute-start.2 = (bf16[512,768]{1,0:T(8,128)(2,1)}, bf16[512,768]{1,0:T(8,128)(2,1)S(1)}, u32[]{:S(2)}, u32[]{:S(2)}) collective-permute-start(bf16[512,768]{1,0:T(8,128)(2,1)} %get-tuple-element.34), channel_id=1, source_target_pairs={{0,8},{8,0},{16,24},{24,16},{32,40},{40,32},{48,56},{56,48},{64,72... | collective-permute-start | bytes 2359304 | tf_op jit(solution)/shard_map/ppermute | solution.py:39
  152.2 27.5 %all-to-all-start.4 = ((bf16[16,8,896]{2,1,0:T(8,128)(2,1)}), bf16[16,8,896]{2,1,0:T(8,128)(2,1)S(1)}, u32[]{:S(2)}, u32[]{:S(2)}) async-start(bf16[16,8,896]{2,1,0:T(8,128)(2,1)} %bitcast.11), calls=%async_computation.4 | async-start | bytes 458752 | tf_op jit(solution)/shard_map/all_to_all | solution.py:43
  162.7 12.8 %collective-permute-start.3 = (bf16[256,768]{1,0:T(8,128)(2,1)S(1)}, bf16[256,768]{1,0:T(8,128)(2,1)S(1)}, u32[]{:S(2)}, u32[]{:S(2)}) collective-permute-start(bf16[256,768]{1,0:T(8,128)(2,1)S(1)} %slice.31), channel_id=1, source_target_pairs={{0,16},{8,24},{16,0},{24,8},{32,48},{40,56},{48,32},{56,40},{64,80... | collective-permute-start | bytes 1179656 | tf_op jit(solution)/shard_map/ppermute | solution.py:39
  179.7 54.2 %all-to-all-start.5 = ((bf16[16,16,768]{2,1,0:T(8,128)(2,1)}), bf16[16,16,768]{2,1,0:T(8,128)(2,1)S(1)}, u32[]{:S(2)}, u32[]{:S(2)}) async-start(bf16[16,16,768]{2,1,0:T(8,128)(2,1)} %bitcast.12), calls=%async_computation.5 | async-start | bytes 786432 | tf_op jit(solution)/shard_map/all_to_all | solution.py:43
  188.1 3.1 %collective-permute-start.4 = (f32[8,896]{1,0:T(8,128)S(1)}, f32[8,896]{1,0:T(8,128)S(1)}, u32[]{:S(2)}, u32[]{:S(2)}) collective-permute-start(f32[8,896]{1,0:T(8,128)S(1)} %convert_reduce_fusion.1), channel_id=1, source_target_pairs={{0,8},{8,0},{16,24},{24,16},{32,40},{40,32},{48,56},{56,48},{64,72... | collective-permute-start | bytes 86024 | tf_op jit(solution)/shard_map/ppermute | solution.py:39
  191.2 5.8 %collective-permute-start.5 = (f32[8,896]{1,0:T(8,128)S(1)}, f32[8,896]{1,0:T(8,128)S(1)}, u32[]{:S(2)}, u32[]{:S(2)}) collective-permute-start(f32[8,896]{1,0:T(8,128)S(1)} %add.32), channel_id=1, source_target_pairs={{0,16},{8,24},{16,0},{24,8},{32,48},{40,56},{48,32},{56,40},{64,80... | collective-permute-start | bytes 86024 | tf_op jit(solution)/shard_map/ppermute | solution.py:39

commit v5 on v4

--- a/solution.py
+++ b/solution.py
@@ -385,7 +385,7 @@
     part = jnp.sum(part.astype(F32), axis=0)
     part = part + permute(part, to_core)
     part = part + permute(part, to_xlo)
-    whole = gather(part, "dp", Z_GROUPS).reshape(16, 8, 896)
+    whole = gather(part.astype(BF), "dp", Z_GROUPS).reshape(16, 8, 896).astype(F32)
     grad_head = jnp.transpose(whole[:, :, :768].reshape(128, 768))
     grad_gain = whole[:, 0, 768:816].reshape(768)
     return (grad_proj, grad_head, grad_gain, features)

time: 236 us -> 234 us (level)
  no operation moved by 1% of the time
where the time goes in v5:
time: 234 us; the launch traced here: 233 us
  blocking collectives  77.1 us (33%)
  starting transfers between devices  69.3 us (30%)
  waiting for transfers between devices  51.2 us (22%)
  Pallas kernels  18.7 us (8%)
  local copies, waits for them, and re-layouts  11.5 us (5%)
  other arithmetic  4.46 us (2%)
    all_gather x3, blocking collectives, gather(): return lax.all_gather(x, axis, axis=0, tiled=True, axis_index_groups=groups)  77.1 us
    all_to_all x6, starting transfers between devices, exchange(): lax.all_to_all(x, axis, split_axis=0, concat_axis=0, tiled=True, axis_ind...  54.4 us
    all_to_all x6, waiting for transfers between devices, exchange(): lax.all_to_all(x, axis, split_axis=0, concat_axis=0, tiled=True, axis_ind...  30 us
    ppermute x6, waiting for transfers between devices, permute(): return lax.ppermute(x, 'dp', [(i, target(i)) for i in range(N_DP)])  21.1 us
    ppermute x6, starting transfers between devices, permute(): return lax.ppermute(x, 'dp', [(i, target(i)) for i in range(N_DP)])  14.9 us
    pallas_call x3, Pallas kernels, call(): pl.pallas_call(kernel, out_shape=outs, in_specs=specs, out_specs=jax.tree...  13.8 us
  transfers between devices with their start and end apart: 12, of which 9 were waited for; matrix products, arithmetic and copies ran while one was open for 3% of the time, Pallas kernels for 0%

profile of v5, /device:TPU:2, one launch (start us, length us, event | category | flops | bytes accessed | tf_op | source)
XLA Modules:
  0.0 233.1 jit_solution(10436827456450207851)
XLA Ops:
  0.6 0.0 copy-start.7
  0.7 0.6 pad_add_fusion.1.position_ref
  1.2 2.8 %cut_windows.1 = bf16[2,64,640]{2,1,0:T(8,128)(2,1)} custom-call(s32[2]{0:T(128)} %pad_add_fusion.1.position_ref, s32[1,128]{1,0:T(1,128)} %bitcast.29, s32[1,128]{1,0:T(1,128)} %bitcast.27, s32[1,128]{1,0:T(1,128)} %bitcast.28, bf16[8,512,128]{2,1,0:T(8,128)(2,1)} %latents_ref.1, bf16[8,512,128]{2,1,0:T(8,128)(2,1)} %labels_ref.1), custom_call_target="tpu_custom_call" | custom-call | tf_op jit(solution)/shard_map/cut_windows/pallas_call | solution.py:106
  4.0 1.8 copy.17
  5.8 17.1 %all-to-all-start = ((bf16[64,2,640]{2,1,0:T(2,128)(2,1)}), bf16[64,2,640]{2,1,0:T(2,128)(2,1)S(1)}, u32[]{:S(2)}, u32[]{:S(2)}) async-start(bf16[64,2,640]{2,1,0:T(2,128)(2,1)} %copy.17), calls=%async_computation | async-start | bytes 327680 | tf_op jit(solution)/shard_map/all_to_all | solution.py:43
  22.9 23.6 %all_gather.9 = bf16[64,768]{1,0:T(8,128)(2,1)S(1)} all-gather(bf16[16,768]{1,0:T(8,128)(2,1)S(1)} %copy-done.5), channel_id=1, replica_groups={{0,128,256,384},{8,136,264,392},{16,144,272,400},{24,152,280,408},{32,1..., dimensions={0}, use_global_device_ids=true | all-gather | bytes 122880 | tf_op jit(solution)/shard_map/all_gather | solution.py:49
  46.5 0.1 reshape.44
  46.5 0.9 gather_fusion
  47.4 0.7 reshape.45
  48.2 8.8 %all-to-all-start.1 = ((bf16[64,2,640]{2,1,0:T(2,128)(2,1)}), bf16[64,2,640]{2,1,0:T(2,128)(2,1)S(1)}, u32[]{:S(2)}, u32[]{:S(2)}) async-start(bf16[64,2,640]{2,1,0:T(2,128)(2,1)} %reshape.45), calls=%async_computation.1 | async-start | bytes 327680 | tf_op jit(solution)/shard_map/all_to_all | solution.py:43
  56.9 2.4 %collective-permute-start = (bf16[64,768]{1,0:T(8,128)(2,1)S(1)}, bf16[64,768]{1,0:T(8,128)(2,1)S(1)}, u32[]{:S(2)}, u32[]{:S(2)}) collective-permute-start(bf16[64,768]{1,0:T(8,128)(2,1)S(1)} %all_gather.9), channel_id=1, source_target_pairs={{0,16},{8,24},{16,0},{24,8},{32,48},{40,56},{48,32},{56,40},{64,80... | collective-permute-start | bytes 294920 | tf_op jit(solution)/shard_map/ppermute | solution.py:39
  59.3 4.8 %collective-permute-done = bf16[64,768]{1,0:T(8,128)(2,1)S(1)} collective-permute-done((bf16[64,768]{1,0:T(8,128)(2,1)S(1)}, bf16[64,768]{1,0:T(8,128)(2,1)S(1)}, u32[]{:S(2)}, u32[]{:S(2)}) %collective-permute-start) | collective-permute-done | bytes 98336 | tf_op jit(solution)/shard_map/ppermute | solution.py:39
  64.2 19.7 %all_gather.10 = bf16[512,768]{1,0:T(8,128)(2,1)S(1)} all-gather(bf16[128,768]{1,0:T(8,128)(2,1)S(1)} %pad_maximum_fusion), channel_id=1, replica_groups={{0,32,64,96},{8,40,72,104},{16,48,80,112},{24,56,88,120},{128,160,192,2..., dimensions={0}, use_global_device_ids=true | all-gather | bytes 983040 | tf_op jit(solution)/shard_map/all_gather | solution.py:49
  83.9 0.0 all-to-all-done.1
  83.9 0.7 copy.22
  84.6 2.1 order_rows.1
  86.8 6.2 %all-to-all-start.2 = ((bf16[8,640,128]{2,1,0:T(8,128)(2,1)}), bf16[8,640,128]{2,1,0:T(8,128)(2,1)S(1)}, u32[]{:S(2)}, u32[]{:S(2)}) async-start(bf16[8,640,128]{2,1,0:T(8,128)(2,1)} %order_rows.1), calls=%async_computation.2 | async-start | bytes 2621440 | tf_op jit(solution)/shard_map/all_to_all | solution.py:43
  92.9 1.9 collective-permute-start.1
  94.9 0.6 reshape.47.gain_ref
  95.5 0.7 pad_add_fusion.place_ref
  96.1 1.0 collective-permute-done.1.core_ref
  97.1 12.3 %all-to-all-done.2.gathered_ref = bf16[8,640,128]{2,1,0:T(8,128)(2,1)S(1)} async-done(((bf16[8,640,128]{2,1,0:T(8,128)(2,1)}), bf16[8,640,128]{2,1,0:T(8,128)(2,1)S(1)}, u32[]{:S(2)}, u32[]{:S(2)}) %all-to-all-start.2) | async-done | bytes 1310752 | tf_op jit(solution)/shard_map/all_to_all | solution.py:43
  109.4 1.1 copy-done
  110.5 5.1 %forward.1 = (bf16[8,640,128]{2,1,0:T(8,128)(2,1)}, f32[512,768]{1,0:T(8,128)}, bf16[512,1024]{1,0:T(8,128)(2,1)}) custom-call(s32[2]{0:T(128)} %pad_add_fusion.place_ref, bf16[8,640,128]{2,1,0:T(8,128)(2,1)} %copy-done, bf16[4,2,4,16,768]{4,3,2,1,0:T(8,128)(2,1)} %bitcast.24, bf16[4,2,4,16,768]{4,3,2,1,0:T(8,128)(2,1)} %copy-done.4, ...), custom_call_target="tpu_custom_call" | custom-call | tf_op jit(solution)/shard_map/forward/pallas_call | solution.py:314
  115.5 3.7 %all-to-all-start.3 = ((bf16[8,640,128]{2,1,0:T(8,128)(2,1)}), bf16[8,640,128]{2,1,0:T(8,128)(2,1)S(1)}, u32[]{:S(2)}, u32[]{:S(2)}) async-start(bf16[8,640,128]{2,1,0:T(8,128)(2,1)} %get-tuple-element.28), calls=%async_computation.3 | async-start | bytes 2621440 | tf_op jit(solution)/shard_map/all_to_all | solution.py:43
  119.2 1.3 copy.19
  120.6 1.6 slice.23.labels_ref
  122.1 14.3 %all-to-all-done.3.sent_ref = bf16[8,640,128]{2,1,0:T(8,128)(2,1)S(1)} async-done(((bf16[8,640,128]{2,1,0:T(8,128)(2,1)}), bf16[8,640,128]{2,1,0:T(8,128)(2,1)S(1)}, u32[]{:S(2)}, u32[]{:S(2)}) %all-to-all-start.3) | async-done | bytes 1310752 | tf_op jit(solution)/shard_map/all_to_all | solution.py:43
  136.4 1.1 copy-done.1
  137.5 5.2 %backward.1 = (bf16[512,768]{1,0:T(8,128)(2,1)}, bf16[512,768]{1,0:T(8,128)(2,1)}, bf16[128,896]{1,0:T(8,128)(2,1)}) custom-call(bf16[8,640,128]{2,1,0:T(8,128)(2,1)} %copy-done.1, bf16[8,64,128]{2,1,0:T(8,128)(2,1)} %slice.23.labels_ref, f32[512,768]{1,0:T(8,128)} %get-tuple-element.29.hidden_ref, f32[1,768]{1,0:T(1,128)} %reshape.47.gain_ref, ...), custom_call_target="tpu_custom_call" | custom-call | tf_op jit(solution)/shard_map/backward/pallas_call | solution.py:314
  142.7 3.6 %weight.1 = (f32[512,768]{1,0:T(8,128)}, bf16[512,768]{1,0:T(8,128)(2,1)}) custom-call(s32[2]{0:T(128)} %pad_add_fusion.place_ref, bf16[1024,512]{1,0:T(8,128)(2,1)} %bitcast.22, bf16[512,768]{1,0:T(8,128)(2,1)} %get-tuple-element.32.back_ref), custom_call_target="tpu_custom_call" | custom-call | tf_op jit(solution)/shard_map/weight/pallas_call | solution.py:314
  146.3 1.9 collective-permute-start.2
  148.2 2.5 %collective-permute-done.2 = bf16[512,768]{1,0:T(8,128)(2,1)S(1)} collective-permute-done((bf16[512,768]{1,0:T(8,128)(2,1)}, bf16[512,768]{1,0:T(8,128)(2,1)S(1)}, u32[]{:S(2)}, u32[]{:S(2)}) %collective-permute-start.2) | collective-permute-done | bytes 786464 | tf_op jit(solution)/shard_map/ppermute | solution.py:39
  150.6 1.6 convert_add_fusion
  152.2 10.4 %all-to-all-start.4 = ((bf16[16,8,896]{2,1,0:T(8,128)(2,1)}), bf16[16,8,896]{2,1,0:T(8,128)(2,1)S(1)}, u32[]{:S(2)}, u32[]{:S(2)}) async-start(bf16[16,8,896]{2,1,0:T(8,128)(2,1)} %bitcast.11), calls=%async_computation.4 | async-start | bytes 458752 | tf_op jit(solution)/shard_map/all_to_all | solution.py:43
  162.7 3.4 %collective-permute-start.3 = (bf16[256,768]{1,0:T(8,128)(2,1)S(1)}, bf16[256,768]{1,0:T(8,128)(2,1)S(1)}, u32[]{:S(2)}, u32[]{:S(2)}) collective-permute-start(bf16[256,768]{1,0:T(8,128)(2,1)S(1)} %slice.31), channel_id=1, source_target_pairs={{0,16},{8,24},{16,0},{24,8},{32,48},{40,56},{48,32},{56,40},{64,80... | collective-permute-start | bytes 1179656 | tf_op jit(solution)/shard_map/ppermute | solution.py:39
  166.1 9.4 %collective-permute-done.3 = bf16[256,768]{1,0:T(8,128)(2,1)S(1)} collective-permute-done((bf16[256,768]{1,0:T(8,128)(2,1)S(1)}, bf16[256,768]{1,0:T(8,128)(2,1)S(1)}, u32[]{:S(2)}, u32[]{:S(2)}) %collective-permute-start.3) | collective-permute-done | bytes 393248 | tf_op jit(solution)/shard_map/ppermute | solution.py:39
  175.4 0.8 convert_add_fusion.1
  176.3 3.5 %all-to-all-done.4 = bf16[16,8,896]{2,1,0:T(8,128)(2,1)S(1)} async-done(((bf16[16,8,896]{2,1,0:T(8,128)(2,1)}), bf16[16,8,896]{2,1,0:T(8,128)(2,1)S(1)}, u32[]{:S(2)}, u32[]{:S(2)}) %all-to-all-start.4) | async-done | bytes 229408 | tf_op jit(solution)/shard_map/all_to_all | solution.py:43
  179.7 8.3 %all-to-all-start.5 = ((bf16[16,16,768]{2,1,0:T(8,128)(2,1)}), bf16[16,16,768]{2,1,0:T(8,128)(2,1)S(1)}, u32[]{:S(2)}, u32[]{:S(2)}) async-start(bf16[16,16,768]{2,1,0:T(8,128)(2,1)} %bitcast.12), calls=%async_computation.5 | async-start | bytes 786432 | tf_op jit(solution)/shard_map/all_to_all | solution.py:43
  188.1 1.9 collective-permute-start.4
  190.0 1.2 collective-permute-done.4
  191.2 3.4 %collective-permute-start.5 = (f32[8,896]{1,0:T(8,128)S(1)}, f32[8,896]{1,0:T(8,128)S(1)}, u32[]{:S(2)}, u32[]{:S(2)}) collective-permute-start(f32[8,896]{1,0:T(8,128)S(1)} %add.32), channel_id=1, source_target_pairs={{0,16},{8,24},{16,0},{24,8},{32,48},{40,56},{48,32},{56,40},{64,80... | collective-permute-start | bytes 86024 | tf_op jit(solution)/shard_map/ppermute | solution.py:39
  194.6 2.4 %collective-permute-done.5 = f32[8,896]{1,0:T(8,128)S(1)} collective-permute-done((f32[8,896]{1,0:T(8,128)S(1)}, f32[8,896]{1,0:T(8,128)S(1)}, u32[]{:S(2)}, u32[]{:S(2)}) %collective-permute-start.5) | collective-permute-done | bytes 28704 | tf_op jit(solution)/shard_map/ppermute | solution.py:39
  196.9 33.8 %all_gather.11 = bf16[128,896]{1,0:T(8,128)(2,1)S(1)} all-gather(bf16[8,896]{1,0:T(8,128)(2,1)S(1)} %add_convert_fusion), channel_id=1, replica_groups={{0,32,64,96,128,160,192,224,256,288,320,352,384,416,448,480},{8,40,72,1..., dimensions={0}, use_global_device_ids=true | all-gather | bytes 243712 | tf_op jit(solution)/shard_map/all_gather | solution.py:49
  230.8 0.9 copy.20
  231.8 0.7 reshape_squeeze.3
  232.4 0.7 convert_reduce_fusion
  (25 shorter events, 0.2 us)
Async XLA Ops:
  0.6 45.8 %copy-start.7 = (s32[128]{0:T(128)S(1)}, s32[128]{0:T(128)}, u32[]{:S(2)}) copy-start(s32[128]{0:T(128)} %param.10) | copy-start | bytes 1540
  0.6 22.2 %copy-start.5 = (bf16[16,768]{1,0:T(8,128)(2,1)S(1)}, bf16[16,768]{1,0:T(8,128)(2,1)}, u32[]{:S(2)}) copy-start(bf16[16,768]{1,0:T(8,128)(2,1)} %param.13) | copy-start | bytes 73732
  5.8 40.7 %all-to-all-start = ((bf16[64,2,640]{2,1,0:T(2,128)(2,1)}), bf16[64,2,640]{2,1,0:T(2,128)(2,1)S(1)}, u32[]{:S(2)}, u32[]{:S(2)}) async-start(bf16[64,2,640]{2,1,0:T(2,128)(2,1)} %copy.17), calls=%async_computation | async-start | bytes 327680 | tf_op jit(solution)/shard_map/all_to_all | solution.py:43
  48.2 35.8 %all-to-all-start.1 = ((bf16[64,2,640]{2,1,0:T(2,128)(2,1)}), bf16[64,2,640]{2,1,0:T(2,128)(2,1)S(1)}, u32[]{:S(2)}, u32[]{:S(2)}) async-start(bf16[64,2,640]{2,1,0:T(2,128)(2,1)} %reshape.45), calls=%async_computation.1 | async-start | bytes 327680 | tf_op jit(solution)/shard_map/all_to_all | solution.py:43
  56.9 7.2 %collective-permute-start = (bf16[64,768]{1,0:T(8,128)(2,1)S(1)}, bf16[64,768]{1,0:T(8,128)(2,1)S(1)}, u32[]{:S(2)}, u32[]{:S(2)}) collective-permute-start(bf16[64,768]{1,0:T(8,128)(2,1)S(1)} %all_gather.9), channel_id=1, source_target_pairs={{0,16},{8,24},{16,0},{24,8},{32,48},{40,56},{48,32},{56,40},{64,80... | collective-permute-start | bytes 294920 | tf_op jit(solution)/shard_map/ppermute | solution.py:39
  83.9 9.0 %copy-start.2 = (bf16[512,768]{1,0:T(8,128)(2,1)}, bf16[512,768]{1,0:T(8,128)(2,1)S(1)}, u32[]{:S(2)}) copy-start(bf16[512,768]{1,0:T(8,128)(2,1)S(1)} %all_gather.10) | copy-start | bytes 2359300
  86.8 8.1 %copy-start.6 = (f32[768]{0:T(1024)S(1)}, f32[768]{0:T(1024)}, u32[]{:S(2)}) copy-start(f32[768]{0:T(1024)} %param.14) | copy-start | bytes 9220
  86.8 22.6 %all-to-all-start.2 = ((bf16[8,640,128]{2,1,0:T(8,128)(2,1)}), bf16[8,640,128]{2,1,0:T(8,128)(2,1)S(1)}, u32[]{:S(2)}, u32[]{:S(2)}) async-start(bf16[8,640,128]{2,1,0:T(8,128)(2,1)} %order_rows.1), calls=%async_computation.2 | async-start | bytes 2621440 | tf_op jit(solution)/shard_map/all_to_all | solution.py:43
  92.9 4.2 %collective-permute-start.1 = (bf16[4,2,4,16,768]{4,3,2,1,0:T(8,128)(2,1)S(1)}, bf16[4,2,4,16,768]{4,3,2,1,0:T(8,128)(2,1)S(1)}, u32[]{:S(2)}, u32[]{:S(2)}) collective-permute-start(bf16[4,2,4,16,768]{4,3,2,1,0:T(8,128)(2,1)S(1)} %bitcast.23), channel_id=1, source_target_pairs={{0,8},{8,0},{16,24},{24,16},{32,40},{40,32},{48,56},{56,48},{64,72... | collective-permute-start | bytes 2359304 | tf_op jit(solution)/shard_map/ppermute | solution.py:39
  97.1 12.3 %copy-start.4 = (bf16[4,2,4,16,768]{4,3,2,1,0:T(8,128)(2,1)}, bf16[4,2,4,16,768]{4,3,2,1,0:T(8,128)(2,1)S(1)}, u32[]{:S(2)}) copy-start(bf16[4,2,4,16,768]{4,3,2,1,0:T(8,128)(2,1)S(1)} %collective-permute-done.1.core_ref) | copy-start | bytes 2359300
  109.4 1.1 copy-start
  115.5 3.7 %copy-start.3 = (bf16[512,1024]{1,0:T(8,128)(2,1)S(1)}, bf16[512,1024]{1,0:T(8,128)(2,1)}, u32[]{:S(2)}) copy-start(bf16[512,1024]{1,0:T(8,128)(2,1)} %get-tuple-element.31) | copy-start | bytes 3145732
  115.5 20.9 %all-to-all-start.3 = ((bf16[8,640,128]{2,1,0:T(8,128)(2,1)}), bf16[8,640,128]{2,1,0:T(8,128)(2,1)S(1)}, u32[]{:S(2)}, u32[]{:S(2)}) async-start(bf16[8,640,128]{2,1,0:T(8,128)(2,1)} %get-tuple-element.28), calls=%async_computation.3 | async-start | bytes 2621440 | tf_op jit(solution)/shard_map/all_to_all | solution.py:43
  136.4 1.1 copy-start.1
  146.3 4.4 %collective-permute-start.2 = (bf16[512,768]{1,0:T(8,128)(2,1)}, bf16[512,768]{1,0:T(8,128)(2,1)S(1)}, u32[]{:S(2)}, u32[]{:S(2)}) collective-permute-start(bf16[512,768]{1,0:T(8,128)(2,1)} %get-tuple-element.34), channel_id=1, source_target_pairs={{0,8},{8,0},{16,24},{24,16},{32,40},{40,32},{48,56},{56,48},{64,72... | collective-permute-start | bytes 2359304 | tf_op jit(solution)/shard_map/ppermute | solution.py:39
  152.2 27.5 %all-to-all-start.4 = ((bf16[16,8,896]{2,1,0:T(8,128)(2,1)}), bf16[16,8,896]{2,1,0:T(8,128)(2,1)S(1)}, u32[]{:S(2)}, u32[]{:S(2)}) async-start(bf16[16,8,896]{2,1,0:T(8,128)(2,1)} %bitcast.11), calls=%async_computation.4 | async-start | bytes 458752 | tf_op jit(solution)/shard_map/all_to_all | solution.py:43
  162.7 12.8 %collective-permute-start.3 = (bf16[256,768]{1,0:T(8,128)(2,1)S(1)}, bf16[256,768]{1,0:T(8,128)(2,1)S(1)}, u32[]{:S(2)}, u32[]{:S(2)}) collective-permute-start(bf16[256,768]{1,0:T(8,128)(2,1)S(1)} %slice.31), channel_id=1, source_target_pairs={{0,16},{8,24},{16,0},{24,8},{32,48},{40,56},{48,32},{56,40},{64,80... | collective-permute-start | bytes 1179656 | tf_op jit(solution)/shard_map/ppermute | solution.py:39
  179.7 52.7 %all-to-all-start.5 = ((bf16[16,16,768]{2,1,0:T(8,128)(2,1)}), bf16[16,16,768]{2,1,0:T(8,128)(2,1)S(1)}, u32[]{:S(2)}, u32[]{:S(2)}) async-start(bf16[16,16,768]{2,1,0:T(8,128)(2,1)} %bitcast.12), calls=%async_computation.5 | async-start | bytes 786432 | tf_op jit(solution)/shard_map/all_to_all | solution.py:43
  188.1 3.1 %collective-permute-start.4 = (f32[8,896]{1,0:T(8,128)S(1)}, f32[8,896]{1,0:T(8,128)S(1)}, u32[]{:S(2)}, u32[]{:S(2)}) collective-permute-start(f32[8,896]{1,0:T(8,128)S(1)} %convert_reduce_fusion.1), channel_id=1, source_target_pairs={{0,8},{8,0},{16,24},{24,16},{32,40},{40,32},{48,56},{56,48},{64,72... | collective-permute-start | bytes 86024 | tf_op jit(solution)/shard_map/ppermute | solution.py:39
  191.2 5.8 %collective-permute-start.5 = (f32[8,896]{1,0:T(8,128)S(1)}, f32[8,896]{1,0:T(8,128)S(1)}, u32[]{:S(2)}, u32[]{:S(2)}) collective-permute-start(f32[8,896]{1,0:T(8,128)S(1)} %add.32), channel_id=1, source_target_pairs={{0,16},{8,24},{16,0},{24,8},{32,48},{40,56},{48,32},{56,40},{64,80... | collective-permute-start | bytes 86024 | tf_op jit(solution)/shard_map/ppermute | solution.py:39
